TPU v7x, 512 devices: a whole 4x4x16 slice. The times are simulated.
512 devices in a mesh: dp: 64 (over y, z), fsdp: 8 (over x, core).
Axes of the slice: x: 4, y: 4, z: 16, core: 2. Of those that a mesh axis runs over, the one named last changes fastest.
Arguments:
- gradient: float32 [64, 3072, 1024], P('dp', 'fsdp'), may hold values from -64 to 64
- residual: float32 [64, 3072, 1024], P('dp', 'fsdp'), may hold values from -3 to 3
- sign_flips: int32 [3072, 1024], P('fsdp'), may hold values from -1 to 1, as said below
- level_table: int32 [16], replicated, may hold values from 0 to 124, as said below
Outputs:
- mean_gradient: float32 [3072, 1024], P('fsdp')
- new_residual: float32 [64, 3072, 1024], P('dp', 'fsdp')
Inputs may be any that keep to these rules, and one draw needn't show every extreme that they name: `sign_flips`: each entry is -1 or 1. `level_table`: first entry 0, last entry 124, strictly increasing, consecutive entries differ by 4 to 12.
All inputs are finite; a program needn't handle non-finite values. Where the computation divides by a largest or mean magnitude, that divisor is 1e-20 or more.
Results may differ from a plain program's by a relative error of at most 0.0028.
Values may be sent and summed in bfloat16 or wider, within the bound.
No kernel may reach another device: no remote copies, remote signals or barrier semaphores. Data moves between devices by JAX's collectives and lax.ppermute only.
A program may use at most 64 MiB of HBM per device.

v0:
```python
import math

import jax
import jax.numpy as jnp
from jax import lax
from jax.sharding import PartitionSpec as P


def hadamard_table(width):
    row_index = lax.broadcasted_iota(jnp.int32, (width, width), 0)
    col_index = lax.broadcasted_iota(jnp.int32, (width, width), 1)
    common = jnp.bitwise_and(row_index, col_index)
    parity = jnp.zeros((width, width), jnp.int32)
    for bit_place in range(width.bit_length()):
        parity = parity + jnp.bitwise_and(jnp.right_shift(common, bit_place), 1)
    parity = jnp.bitwise_and(parity, 1)
    return (1 - 2 * parity).astype(jnp.float32)


def soft_code(offset, centred, levels_count):
    numer = jnp.zeros_like(offset)
    denom = jnp.zeros_like(offset)
    for level in range(levels_count):
        gap = offset - centred[level]
        weight = jnp.exp(-gap * gap / 72.0)
        numer = numer + weight * centred[level]
        denom = denom + weight
    return numer / denom


def on_device(gradient, residual, sign_flips, level_table):
    width = gradient.shape[2]
    replicas = lax.axis_size("dp")
    root = math.sqrt(width)
    walsh_matrix = hadamard_table(width)
    flips = sign_flips.astype(jnp.float32)
    levels = level_table.astype(jnp.float32)
    bottom = levels[0]
    upper = levels[level_table.shape[0] - 1]
    middle = (bottom + upper) / 2.0
    half_span = (upper - bottom) / 2.0
    centred = levels - middle
    rotated = (
        jnp.dot(
            gradient[0] * flips,
            walsh_matrix,
            precision=lax.Precision.HIGHEST,
            preferred_element_type=jnp.float32,
        )
        / root
        + residual[0]
    )
    peak_value = lax.pmax(jnp.max(jnp.abs(rotated)), ("dp", "fsdp")) + 1e-06
    code_full = soft_code(rotated * half_span / peak_value, centred, level_table.shape[0])
    new_residual = rotated - code_full * peak_value / half_span
    codes = code_full.astype(jnp.bfloat16)
    total = lax.psum_scatter(codes.astype(jnp.float32), "dp", scatter_dimension=0, tiled=True)
    factor = peak_value / (half_span * replicas)
    rows = (
        jnp.dot(
            lax.all_gather(total, "dp", axis=0, tiled=True) * factor,
            walsh_matrix,
            precision=lax.Precision.HIGHEST,
            preferred_element_type=jnp.float32,
        )
        / root
    )
    mean_gradient = rows * flips
    return (mean_gradient, new_residual[None])


def solution(mesh):
    placed = (P("dp", "fsdp", None), P("dp", "fsdp", None), P("fsdp", None), P())
    return jax.shard_map(
        on_device,
        mesh=mesh,
        in_specs=placed,
        out_specs=(P("fsdp", None), P("dp", "fsdp", None)),
        check_vma=False,
    )
```

profile of v0, /device:TPU:6, one launch (start us, length us, event | category | flops | bytes accessed | tf_op | source)
XLA Modules:
  0.0 533.2 jit_solution(2220953410066097290)
XLA Ops:
  7.2 0.7 convert_element_type.19
  7.9 0.6 fusion.65
  11.0 0.7 broadcast_subtract_fusion
  11.7 0.7 fusion.64
  12.4 14.0 %abs_reduce_fusion = (f32[]{:T(128)}, f32[384,1024]{1,0:T(8,128)S(1)}) fusion(f32[1,384,1024]{2,1,0:T(8,128)} %param.5, f32[1,384,1024]{2,1,0:T(8,128)} %param.4, s32[384,1024]{1,0:T(8,128)} %param.6), kind=kOutput, calls=%fused_computation.58 | convolution fusion | flops 4872994816 | bytes 6291460 | tf_op jit(solution)/shard_map/dot_general | solution.py:44
  26.4 108.3 %pmax.7 = f32[]{:T(128)} all-reduce(f32[]{:T(128)} %get-tuple-element.22), channel_id=1, replica_groups=mesh['dp'=64,'fsdp'=8] {'dp','fsdp'}, use_global_device_ids=true, to_apply=%region_1.0 | all-reduce | flops 1 | bytes 8 | tf_op jit(solution)/shard_map/pmax | solution.py:53
  135.4 18.5 %subtract_bitcast_fusion = (f32[1,384,1024]{2,1,0:T(8,128)}, bf16[384,1024]{1,0:T(8,128)(2,1)S(1)}) fusion(f32[384,1024]{1,0:T(8,128)S(1)} %get-tuple-element.23, f32[]{:T(128)S(6)} %add.163, f32[]{:T(128)} %bitcast.2, f32[]{:T(128)} %bitcast.19, f32[]{:T(128)} %bitcast.18, f32[]{:T(128)} %bitcast.17, f32[]{:T(128)} %bitcast.16, f32[]{:T(128)} %bitcast.15, ...), kind=kLoop, calls=%fused_computation.55 | loop fusion | flops 46006272 | bytes 3932232 | tf_op jit(solution)/shard_map/broadcast_in_dim | solution.py:69
  153.9 0.2 convert_element_type.44
  154.0 154.8 %fusion = f32[8,1024]{1,0:T(8,128)S(1)} fusion(f32[384,1024]{1,0:T(8,128)S(1)} %convert_element_type.44), kind=kCustom, calls=%all-reduce-scatter | all-reduce-scatter fusion | flops 524289 | bytes 1607680
  308.8 1.3 collective-permute-start.15
  310.1 1.3 collective-permute-start.14
  311.4 1.3 collective-permute-start.13
  312.7 1.3 collective-permute-start.12
  314.0 1.3 collective-permute-start.11
  315.4 1.3 collective-permute-start.10
  316.7 18.7 %collective-permute-start.9 = (f32[8,1024]{1,0:T(8,128)S(1)}, f32[8,1024]{1,0:T(8,128)S(1)}, u32[]{:S(2)}, u32[]{:S(2)}) collective-permute-start(f32[8,1024]{1,0:T(8,128)S(1)} %fusion), channel_id=1, source_target_pairs={{0,80},{8,88},{16,96},{24,104},{32,112},{40,120},{48,128},{56,136}... | collective-permute-start | bytes 98312
  335.4 1.9 collective-permute-start.8
  337.3 9.0 %collective-permute-start.7 = (f32[8,1024]{1,0:T(8,128)S(1)}, f32[8,1024]{1,0:T(8,128)S(1)}, u32[]{:S(2)}, u32[]{:S(2)}) collective-permute-start(f32[8,1024]{1,0:T(8,128)S(1)} %fusion), channel_id=1, source_target_pairs={{0,64},{8,72},{16,80},{24,88},{32,96},{40,104},{48,112},{56,120},{... | collective-permute-start | bytes 98312
  346.3 2.9 collective-permute-start.6
  349.3 6.6 %collective-permute-start.5 = (f32[8,1024]{1,0:T(8,128)S(1)}, f32[8,1024]{1,0:T(8,128)S(1)}, u32[]{:S(2)}, u32[]{:S(2)}) collective-permute-start(f32[8,1024]{1,0:T(8,128)S(1)} %fusion), channel_id=1, source_target_pairs={{0,48},{8,56},{16,64},{24,72},{32,80},{40,88},{48,96},{56,104},{64... | collective-permute-start | bytes 98312
  355.8 1.7 collective-permute-start.4
  357.6 5.4 %collective-permute-start.3 = (f32[8,1024]{1,0:T(8,128)S(1)}, f32[8,1024]{1,0:T(8,128)S(1)}, u32[]{:S(2)}, u32[]{:S(2)}) collective-permute-start(f32[8,1024]{1,0:T(8,128)S(1)} %fusion), channel_id=1, source_target_pairs={{0,32},{8,40},{16,48},{24,56},{32,64},{40,72},{48,80},{56,88},{64,... | collective-permute-start | bytes 98312
  363.0 3.9 collective-permute-start.2
  366.9 1.6 collective-permute-start.1
  368.6 3.3 collective-permute-start
  371.9 1.3 dynamic-slice.4
  373.8 1.7 concatenate
  375.6 0.6 dynamic-slice_bitcast_fusion
  376.3 134.0 %all-gather.3.cloned.1.call-done = f32[64,6,1024]{2,1,0:T(8,128)} async-done(((f32[1,6,1024]{2,1,0:T(8,128)}), f32[64,6,1024]{2,1,0:T(8,128)}) %all-gather.3.cloned.1.call-update) | async-done | bytes 1572880 | tf_op jit(solution)/shard_map/all_gather | solution.py:61
  510.3 1.8 broadcast_multiply_fusion
  512.0 1.4 reshape.15
  513.4 12.9 %multiply_multiply_fusion = f32[384,1024]{1,0:T(8,128)} fusion(s32[384,1024]{1,0:T(8,128)} %param.6, f32[384,1024]{1,0:T(8,128)} %reshape.15), kind=kOutput, calls=%fused_computation.56 | convolution fusion | flops 4871815168 | bytes 4718592 | tf_op jit(solution)/shard_map/dot_general | solution.py:60
  (19 shorter events, 0.1 us)
Async XLA Ops:
  7.2 503.1 %all-gather.3.cloned.1.call-start = ((), (), s32[]{:S(2)}) async-start(), calls=%async_computation | async-start | bytes 2129920 | tf_op jit(solution)/shard_map/all_gather | solution.py:61
  308.8 6.5 %collective-permute-start.15 = (f32[6,1024]{1,0:T(8,128)S(1)}, f32[6,1024]{1,0:T(8,128)S(1)}, u32[]{:S(2)}, u32[]{:S(2)}) collective-permute-start(f32[6,1024]{1,0:T(8,128)S(1)} %slice.88), channel_id=1, source_target_pairs={{0,128},{8,136},{16,144},{24,152},{32,160},{40,168},{48,176},{56,1... | collective-permute-start | bytes 73736
  310.1 6.5 %collective-permute-start.14 = (f32[8,1024]{1,0:T(8,128)S(1)}, f32[8,1024]{1,0:T(8,128)S(1)}, u32[]{:S(2)}, u32[]{:S(2)}) collective-permute-start(f32[8,1024]{1,0:T(8,128)S(1)} %fusion), channel_id=1, source_target_pairs={{0,120},{8,128},{16,136},{24,144},{32,152},{40,160},{48,168},{56,1... | collective-permute-start | bytes 98312
  311.4 24.0 %collective-permute-start.13 = (f32[8,1024]{1,0:T(8,128)S(1)}, f32[8,1024]{1,0:T(8,128)S(1)}, u32[]{:S(2)}, u32[]{:S(2)}) collective-permute-start(f32[8,1024]{1,0:T(8,128)S(1)} %fusion), channel_id=1, source_target_pairs={{0,112},{8,120},{16,128},{24,136},{32,144},{40,152},{48,160},{56,1... | collective-permute-start | bytes 98312
  312.7 24.6 %collective-permute-start.12 = (f32[8,1024]{1,0:T(8,128)S(1)}, f32[8,1024]{1,0:T(8,128)S(1)}, u32[]{:S(2)}, u32[]{:S(2)}) collective-permute-start(f32[8,1024]{1,0:T(8,128)S(1)} %fusion), channel_id=1, source_target_pairs={{0,104},{8,112},{16,120},{24,128},{32,136},{40,144},{48,152},{56,1... | collective-permute-start | bytes 98312
  314.0 32.3 %collective-permute-start.11 = (f32[8,1024]{1,0:T(8,128)S(1)}, f32[8,1024]{1,0:T(8,128)S(1)}, u32[]{:S(2)}, u32[]{:S(2)}) collective-permute-start(f32[8,1024]{1,0:T(8,128)S(1)} %fusion), channel_id=1, source_target_pairs={{0,96},{8,104},{16,112},{24,120},{32,128},{40,136},{48,144},{56,15... | collective-permute-start | bytes 98312
  315.4 33.9 %collective-permute-start.10 = (f32[8,1024]{1,0:T(8,128)S(1)}, f32[8,1024]{1,0:T(8,128)S(1)}, u32[]{:S(2)}, u32[]{:S(2)}) collective-permute-start(f32[8,1024]{1,0:T(8,128)S(1)} %fusion), channel_id=1, source_target_pairs={{0,88},{8,96},{16,104},{24,112},{32,120},{40,128},{48,136},{56,144... | collective-permute-start | bytes 98312
  316.7 39.2 %collective-permute-start.9 = (f32[8,1024]{1,0:T(8,128)S(1)}, f32[8,1024]{1,0:T(8,128)S(1)}, u32[]{:S(2)}, u32[]{:S(2)}) collective-permute-start(f32[8,1024]{1,0:T(8,128)S(1)} %fusion), channel_id=1, source_target_pairs={{0,80},{8,88},{16,96},{24,104},{32,112},{40,120},{48,128},{56,136}... | collective-permute-start | bytes 98312
  335.4 22.2 %collective-permute-start.8 = (f32[8,1024]{1,0:T(8,128)S(1)}, f32[8,1024]{1,0:T(8,128)S(1)}, u32[]{:S(2)}, u32[]{:S(2)}) collective-permute-start(f32[8,1024]{1,0:T(8,128)S(1)} %fusion), channel_id=1, source_target_pairs={{0,72},{8,80},{16,88},{24,96},{32,104},{40,112},{48,120},{56,128},... | collective-permute-start | bytes 98312
  337.3 25.7 %collective-permute-start.7 = (f32[8,1024]{1,0:T(8,128)S(1)}, f32[8,1024]{1,0:T(8,128)S(1)}, u32[]{:S(2)}, u32[]{:S(2)}) collective-permute-start(f32[8,1024]{1,0:T(8,128)S(1)} %fusion), channel_id=1, source_target_pairs={{0,64},{8,72},{16,80},{24,88},{32,96},{40,104},{48,112},{56,120},{... | collective-permute-start | bytes 98312
  346.3 20.6 %collective-permute-start.6 = (f32[8,1024]{1,0:T(8,128)S(1)}, f32[8,1024]{1,0:T(8,128)S(1)}, u32[]{:S(2)}, u32[]{:S(2)}) collective-permute-start(f32[8,1024]{1,0:T(8,128)S(1)} %fusion), channel_id=1, source_target_pairs={{0,56},{8,64},{16,72},{24,80},{32,88},{40,96},{48,104},{56,112},{6... | collective-permute-start | bytes 98312
  349.3 19.3 %collective-permute-start.5 = (f32[8,1024]{1,0:T(8,128)S(1)}, f32[8,1024]{1,0:T(8,128)S(1)}, u32[]{:S(2)}, u32[]{:S(2)}) collective-permute-start(f32[8,1024]{1,0:T(8,128)S(1)} %fusion), channel_id=1, source_target_pairs={{0,48},{8,56},{16,64},{24,72},{32,80},{40,88},{48,96},{56,104},{64... | collective-permute-start | bytes 98312
  355.8 17.9 %collective-permute-start.4 = (f32[8,1024]{1,0:T(8,128)S(1)}, f32[8,1024]{1,0:T(8,128)S(1)}, u32[]{:S(2)}, u32[]{:S(2)}) collective-permute-start(f32[8,1024]{1,0:T(8,128)S(1)} %fusion), channel_id=1, source_target_pairs={{0,40},{8,48},{16,56},{24,64},{32,72},{40,80},{48,88},{56,96},{64,... | collective-permute-start | bytes 98312
  357.6 16.2 %collective-permute-start.3 = (f32[8,1024]{1,0:T(8,128)S(1)}, f32[8,1024]{1,0:T(8,128)S(1)}, u32[]{:S(2)}, u32[]{:S(2)}) collective-permute-start(f32[8,1024]{1,0:T(8,128)S(1)} %fusion), channel_id=1, source_target_pairs={{0,32},{8,40},{16,48},{24,56},{32,64},{40,72},{48,80},{56,88},{64,... | collective-permute-start | bytes 98312
  363.0 10.8 %collective-permute-start.2 = (f32[8,1024]{1,0:T(8,128)S(1)}, f32[8,1024]{1,0:T(8,128)S(1)}, u32[]{:S(2)}, u32[]{:S(2)}) collective-permute-start(f32[8,1024]{1,0:T(8,128)S(1)} %fusion), channel_id=1, source_target_pairs={{0,24},{8,32},{16,40},{24,48},{32,56},{40,64},{48,72},{56,80},{64,... | collective-permute-start | bytes 98312
  366.9 6.9 %collective-permute-start.1 = (f32[8,1024]{1,0:T(8,128)S(1)}, f32[8,1024]{1,0:T(8,128)S(1)}, u32[]{:S(2)}, u32[]{:S(2)}) collective-permute-start(f32[8,1024]{1,0:T(8,128)S(1)} %fusion), channel_id=1, source_target_pairs={{0,16},{8,24},{16,32},{24,40},{32,48},{40,56},{48,64},{56,72},{64,... | collective-permute-start | bytes 98312
  368.6 5.3 collective-permute-start
Sparse Core Ops, SparseCore 0:
  376.4 133.8 all-gather.2
where the time goes:
time: 534 us; the launch traced here: 533 us
  blocking collectives  263 us (49%)
  waiting for transfers between devices  134 us (25%)
  starting transfers between devices  62.8 us (12%)
  matrix products  26.9 us (5%)
  other arithmetic  21.7 us (4%)
  between operations  18.3 us (3%)
  local copies, waits for them, and re-layouts  6.33 us (1%)
    unnamed x1, blocking collectives  155 us
    all_gather x1, waiting for transfers between devices, on_device(): lax.all_gather(total, 'dp', axis=0, tiled=True) * factor  134 us
    pmax x1, blocking collectives, on_device(): peak_value = lax.pmax(jnp.max(jnp.abs(rotated)), ('dp', 'fsdp')) + 1e-06  108 us
    unnamed x16, starting transfers between devices  62.8 us
    broadcast_in_dim x1, other arithmetic, on_device(): return (mean_gradient, new_residual[None])  18.5 us
    dot_general x1, matrix products, on_device(): jnp.dot(gradient[0] * flips, walsh_matrix, precision=lax.Precision.HIGHES...  14 us
    dot_general x1, matrix products, on_device(): jnp.dot(lax.all_gather(total, 'dp', axis=0, tiled=True) * factor, walsh_m...  12.9 us
  transfers between devices with their start and end apart: 17, of which 1 were waited for; matrix products, arithmetic and copies ran while one was open for 0% of the time, Pallas kernels for 0%

commit v1 on v0

v1 whole, which is shorter than its diff:
```python
import functools
import math

import jax
import jax.numpy as jnp
import numpy as np
from jax import lax
from jax.experimental import pallas as pl
from jax.experimental.pallas import tpu as pltpu
from jax.sharding import PartitionSpec as P

F32, BF16, F16 = jnp.float32, jnp.bfloat16, jnp.float16
FOLD = 256
LANES = 128
VMEM_BYTES = 48 * 1024 * 1024


def hadamard(width):
    table = np.ones((1, 1), np.float32)
    while table.shape[0] < width:
        table = np.block([[table, table], [table, -table]])
    return table


def turn(values, matrix, scale):
    count = values.shape[1] // FOLD
    parts = [values[:, k * FOLD : (k + 1) * FOLD] for k in range(count)]
    step = 1
    while step < count:
        nxt = list(parts)
        for k in range(count):
            if not k & step:
                nxt[k] = parts[k] + parts[k + step]
                nxt[k + step] = parts[k] - parts[k + step]
        parts = nxt
        step *= 2
    turned = []
    for part in parts:
        part = part * scale
        high = part.astype(BF16)
        rest = part - high.astype(F32)
        middle = rest.astype(BF16)
        low = (rest - middle.astype(F32)).astype(BF16)
        dot = functools.partial(jnp.dot, preferred_element_type=F32)
        turned.append(dot(high, matrix) + (dot(middle, matrix) + dot(low, matrix)))
    return turned


def rotate_kernel(copies, grad_ref, flip_ref, resid_ref, matrix_ref, rot_ref, peak_ref):
    width = grad_ref.shape[1]
    signed = grad_ref[...] * flip_ref[...].astype(F32)
    turned = turn(signed, matrix_ref[...], 1.0 / math.sqrt(width))
    top = jnp.zeros((8, LANES), F32)
    for k, part in enumerate(turned):
        cols = slice(k * FOLD, (k + 1) * FOLD)
        rotated = part + resid_ref[:, cols]
        rot_ref[:, cols] = rotated
        size = jnp.abs(rotated)
        for at in range(0, FOLD, LANES):
            lane = size[:, at : at + LANES]
            top = jnp.maximum(top, jnp.max(lane.reshape(-1, 8, LANES), axis=0))
    top = jnp.broadcast_to(top[None], (copies, 8, LANES))

    @pl.when(pl.program_id(0) == 0)
    def _():
        peak_ref[...] = top

    @pl.when(pl.program_id(0) > 0)
    def _():
        peak_ref[...] = jnp.maximum(peak_ref[...], top)


def quantize_kernel(levels_ref, peaks_ref, rot_ref, resid_ref, code_ref, peak_ref):
    count = levels_ref.shape[0]
    peak = jnp.max(peaks_ref[...]) + 1e-06
    bottom = levels_ref[0].astype(F32)
    upper = levels_ref[count - 1].astype(F32)
    middle = (bottom + upper) * 0.5
    half_span = (upper - bottom) * 0.5
    log2e = math.log2(math.e)
    centred = [levels_ref[k].astype(F32) - middle for k in range(count)]
    lift = [c * c * (-log2e / 72.0) for c in centred]
    peak_row = jnp.full((1, LANES), peak, F32)
    half_row = jnp.full((1, LANES), half_span, F32)
    reach = half_row / peak_row
    back = peak_row / half_row
    reach = reach[0:1, 0:1] * (log2e / 36.0)
    back = back[0:1, 0:1]
    peak_ref[...] = jnp.full(peak_ref.shape, peak, F32)
    rows, width = rot_ref.shape
    wide = 512
    per_row = width // wide

    def chunk(step, carry):
        row = pl.multiple_of((step // per_row) * 16, 16)
        col = pl.multiple_of((step % per_row) * wide, wide)
        at = (pl.ds(row, 16), pl.ds(col, wide))
        rotated = rot_ref[at]
        place = rotated * reach
        numer = jnp.zeros_like(place)
        denom = jnp.zeros_like(place)
        for k in range(count):
            weight = jnp.exp2(place * centred[k] + lift[k])
            numer = numer + weight * centred[k]
            denom = denom + weight
        code = numer / denom
        resid_ref[at] = rotated - code * back
        code_ref[at] = code.astype(BF16)
        return carry

    lax.fori_loop(0, (rows // 16) * per_row, chunk, 0)


def partial_kernel(codes_ref, matrix_ref, out_ref):
    width = codes_ref.shape[2]
    total = codes_ref[0].astype(F32)
    for k in range(1, codes_ref.shape[0]):
        total = total + codes_ref[k].astype(F32)
    turned = turn(total, matrix_ref[...], 1.0 / math.sqrt(width))
    for k, part in enumerate(turned):
        for at in range(0, FOLD, LANES):
            out_ref[(k * FOLD + at) // LANES] = part[:, at : at + LANES]


def on_device(gradient, residual, sign_flips, level_table):
    _, rows, width = gradient.shape
    replicas = lax.axis_size("dp")
    parts = lax.axis_size("fsdp")
    depth = 16
    ys = replicas // depth
    near = [[y * depth + 2 * h + l for y in range(ys) for l in range(2)] for h in range(depth // 2)]
    far = [[y * depth + 2 * h + l for h in range(depth // 2)] for y in range(ys) for l in range(2)]
    along_y = [[y * depth + z for y in range(ys)] for z in range(depth)]
    along_z = [[y * depth + z for z in range(depth)] for y in range(ys)]
    matrix = jnp.asarray(hadamard(FOLD), BF16)
    params = functools.partial(pltpu.CompilerParams, vmem_limit_bytes=VMEM_BYTES)

    block = 96
    tile = pl.BlockSpec((block, width), lambda i: (i, 0))
    whole = lambda *shape: pl.BlockSpec(shape, lambda i: (0,) * len(shape))
    rotated, peaks = pl.pallas_call(
        functools.partial(rotate_kernel, parts),
        grid=(rows // block,),
        in_specs=[tile, tile, tile, whole(FOLD, FOLD)],
        out_specs=[tile, whole(parts, 8, LANES)],
        out_shape=[
            jax.ShapeDtypeStruct((rows, width), F32),
            jax.ShapeDtypeStruct((parts, 8, LANES), F32),
        ],
        compiler_params=params(),
        name="rotate",
    )(gradient[0], sign_flips, residual[0], matrix)

    def spread(tiles, axis, groups, size):
        top = jnp.max(tiles, axis=0, keepdims=True)
        return lax.all_to_all(
            jnp.broadcast_to(top, (size, 8, LANES)), axis, 0, 0, axis_index_groups=groups
        )

    peaks = lax.all_to_all(peaks, "fsdp", 0, 0)
    peaks = spread(peaks, "dp", along_y, ys)
    peaks = spread(peaks, "dp", along_z, depth)

    new_residual, codes, peak = pl.pallas_call(
        quantize_kernel,
        grid=(rows // block,),
        in_specs=[
            pl.BlockSpec(memory_space=pltpu.SMEM),
            whole(depth, 8, LANES),
            tile,
        ],
        out_specs=[tile, tile, whole(1, LANES)],
        out_shape=[
            jax.ShapeDtypeStruct((rows, width), F32),
            jax.ShapeDtypeStruct((rows, width), BF16),
            jax.ShapeDtypeStruct((1, LANES), F32),
        ],
        compiler_params=params(),
        name="quantize",
    )(level_table, peaks, rotated)

    first, second = len(near[0]), len(far[0])
    share = rows // first
    codes = codes.reshape(first, share, width)
    codes = lax.all_to_all(codes, "dp", 0, 0, axis_index_groups=near)
    partial = pl.pallas_call(
        partial_kernel,
        out_shape=jax.ShapeDtypeStruct((second, share, width // second), F32),
        compiler_params=params(),
        name="partial",
    )(codes, matrix)
    partial = lax.all_to_all(partial.astype(F16), "dp", 0, 0, axis_index_groups=far)
    mean = jnp.sum(partial.astype(F32), axis=0) * 0.125
    mean = jnp.broadcast_to(mean.astype(F16)[None], partial.shape)
    mean = lax.all_to_all(mean, "dp", 0, 0, axis_index_groups=far)
    mean = mean.transpose(1, 0, 2).reshape(share, width)
    mean = jnp.broadcast_to(mean[None], (first, share, width))
    mean = lax.all_to_all(mean, "dp", 0, 0, axis_index_groups=near)
    half_span = (level_table[-1] - level_table[0]).astype(F32) * 0.5
    factor = peak[0, 0] / (half_span * (replicas // 8))
    mean = mean.reshape(rows, width).astype(F32) * factor * sign_flips.astype(F32)
    return mean, new_residual[None]


def solution(mesh):
    placed = (P("dp", "fsdp", None), P("dp", "fsdp", None), P("fsdp", None), P())
    return jax.shard_map(
        on_device,
        mesh=mesh,
        in_specs=placed,
        out_specs=(P("fsdp", None), P("dp", "fsdp", None)),
        check_vma=False,
    )
```

time: 534 us -> 126 us (0.24)
  blocking collectives: 263 us -> 91.9 us
  waiting for transfers between devices: 134 us -> 8.16 us
  starting transfers between devices: 62.8 us -> 3.55 us
  matrix products: 26.9 us -> 0 us
  other arithmetic: 21.7 us -> 1.7 us
  between operations: 18.3 us -> 2 us
  Pallas kernels: 0 us -> 12 us
    unnamed x1 -> x0, blocking collectives: 155 us -> none
    all_gather x1 -> x0, waiting for transfers between devices: 134 us -> none  [on_device(): lax.all_gather(total, 'dp', axis=0, tiled=True) * factor]
    pmax x1 -> x0, blocking collectives: 108 us -> none  [on_device(): peak_value = lax.pmax(jnp.max(jnp.abs(rotated)), ('dp', 'fsdp')) + 1e-06]
    all_to_all x0 -> x6, blocking collectives: none -> 91.9 us  [the longest x2 33.9 us: spread(): lax.all_to_all(jnp.broadcast_to(top, (size, 8, LANES)), axis, 0, 0, axis_...]
    unnamed x16 -> x0, starting transfers between devices: 62.8 us -> none
    dot_general x2 -> x0, matrix products: 26.9 us -> none  [the longest x1 14 us: on_device(): jnp.dot(gradient[0] * flips, walsh_matrix, precision=lax.Precision.HIGHES...]
    broadcast_in_dim x1 -> x0, other arithmetic: 18.5 us -> none  [on_device(): return (mean_gradient, new_residual[None])]
    pallas_call x0 -> x3, Pallas kernels: none -> 12 us  [the longest x1 8.19 us: on_device(): pl.pallas_call(quantize_kernel, grid=(rows // block,), in_specs=[pl.Block...]
  transfers between devices with their start and end apart: 17 -> 1, of which waited for: 1 -> 1; matrix products, arithmetic and copies ran while one was open for 0% -> 0% of each run, Pallas kernels for 0% -> 0%
where the time goes in v1:
time: 126 us; the launch traced here: 125 us
  blocking collectives  91.9 us (73%)
  Pallas kernels  12 us (10%)
  waiting for transfers between devices  8.16 us (6%)
  local copies, waits for them, and re-layouts  5.37 us (4%)
  starting transfers between devices  3.55 us (3%)
  between operations  2 us (2%)
  other arithmetic  1.7 us (1%)
    all_to_all x2, blocking collectives, spread(): lax.all_to_all(jnp.broadcast_to(top, (size, 8, LANES)), axis, 0, 0, axis_...  33.9 us
    all_to_all x1, blocking collectives, on_device(): lax.all_to_all(partial.astype(F16), 'dp', 0, 0, axis_index_groups=far)  17.2 us
    all_to_all x1, blocking collectives, on_device(): mean = lax.all_to_all(mean, 'dp', 0, 0, axis_index_groups=far)  16.4 us
    all_to_all x1, blocking collectives, on_device(): codes = lax.all_to_all(codes, 'dp', 0, 0, axis_index_groups=near)  12.8 us
    all_to_all x1, blocking collectives, on_device(): peaks = lax.all_to_all(peaks, 'fsdp', 0, 0)  11.6 us
    pallas_call x1, Pallas kernels, on_device(): pl.pallas_call(quantize_kernel, grid=(rows // block,), in_specs=[pl.Block...  8.19 us
    all_to_all x1, waiting for transfers between devices, on_device(): mean = lax.all_to_all(mean, 'dp', 0, 0, axis_index_groups=near)  8.16 us
    unnamed x12, local copies, waits for them, and re-layouts  3.73 us
  transfers between devices with their start and end apart: 1, of which 1 were waited for; matrix products, arithmetic and copies ran while one was open for 0% of the time, Pallas kernels for 0%

profile of v1, /device:TPU:6, one launch (start us, length us, event | category | flops | bytes accessed | tf_op | source)
XLA Modules:
  0.0 124.6 jit_solution(8263902240833539370)
XLA Ops:
  0.6 0.0 copy-start
  0.6 1.4 %copy-done = s32[384,1024]{1,0:T(8,128)S(1)} copy-done((s32[384,1024]{1,0:T(8,128)S(1)}, s32[384,1024]{1,0:T(8,128)}, u32[]{:S(2)}) %copy-start) | copy-done | bytes 1572888
  2.0 0.0 copy-start.2
  2.0 1.4 %copy-done.2 = f32[1,384,1024]{2,1,0:T(8,128)S(1)} copy-done((f32[1,384,1024]{2,1,0:T(8,128)S(1)}, f32[1,384,1024]{2,1,0:T(8,128)}, u32[]{:S(2)}) %copy-start.2) | copy-done | bytes 1572888
  3.4 0.0 copy-start.3
  3.5 0.9 copy-done.3
  4.4 0.0 copy-start.5
  4.4 3.4 %rotate.1 = (f32[384,1024]{1,0:T(8,128)S(1)}, f32[8,8,128]{2,1,0:T(8,128)S(1)}) custom-call(f32[384,1024]{1,0:T(8,128)S(1)} %bitcast.15, s32[384,1024]{1,0:T(8,128)S(1)} %copy-done, f32[384,1024]{1,0:T(8,128)} %bitcast.18, bf16[256,256]{1,0:T(8,128)(2,1)S(1)} %copy-done.3), custom_call_target="tpu_custom_call" | custom-call | tf_op jit(solution)/shard_map/rotate/pallas_call | solution.py:141
  7.7 11.6 %all_to_all.35 = f32[8,8,128]{2,1,0:T(8,128)S(1)} all-to-all(f32[8,8,128]{2,1,0:T(8,128)S(1)} %get-tuple-element.7), channel_id=1, replica_groups=mesh['dp'=64,'fsdp'=8] {'fsdp'}, dimensions={0} | all-to-all | bytes 65536 | tf_op jit(solution)/shard_map/all_to_all | solution.py:160
  19.3 7.7 %all_to_all.36 = f32[4,8,128]{2,1,0:T(8,128)S(1)} all-to-all(f32[4,8,128]{2,1,0:T(8,128)S(1)} %broadcast_in_dim.12), channel_id=1, replica_groups={{0,128,256,384},{8,136,264,392},{16,144,272,400},{24,152,280,408},{32,1..., dimensions={0} | all-to-all | bytes 32768 | tf_op jit(solution)/shard_map/all_to_all | solution.py:156
  27.0 26.2 %all_to_all.37.peaks_ref = f32[16,8,128]{2,1,0:T(8,128)S(1)} all-to-all(f32[16,8,128]{2,1,0:T(8,128)S(1)} %broadcast_in_dim.13), channel_id=1, replica_groups={{0,8,16,24,32,40,48,56,64,72,80,88,96,104,112,120},{128,136,144,152,160..., dimensions={0} | all-to-all | bytes 131072 | tf_op jit(solution)/shard_map/all_to_all | solution.py:156
  53.2 0.0 copy-done.5
  53.2 0.0 copy-start.4
  53.2 8.2 %quantize.1 = (f32[384,1024]{1,0:T(8,128)}, bf16[384,1024]{1,0:T(8,128)(2,1)S(1)}, f32[1,128]{1,0:T(1,128)S(1)}) custom-call(s32[16]{0:T(128)S(1)} %copy-done.5, f32[16,8,128]{2,1,0:T(8,128)S(1)} %all_to_all.37.peaks_ref, f32[384,1024]{1,0:T(8,128)S(1)} %get-tuple-element.8.rot_ref), custom_call_target="tpu_custom_call" | custom-call | tf_op jit(solution)/shard_map/quantize/pallas_call | solution.py:164
  61.4 12.8 %all_to_all.38.codes_ref = bf16[8,48,1024]{2,1,0:T(8,128)(2,1)S(1)} all-to-all(bf16[8,48,1024]{2,1,0:T(8,128)(2,1)S(1)} %bitcast.16), channel_id=1, replica_groups={{0,8,128,136,256,264,384,392},{16,24,144,152,272,280,400,408},{32,40,16..., dimensions={0} | all-to-all | bytes 1572864 | tf_op jit(solution)/shard_map/all_to_all | solution.py:185
  74.2 0.0 copy-done.4
  74.2 0.4 partial.1
  74.6 17.2 %all_to_all.39 = f16[8,48,128]{2,1,0:T(8,128)(2,1)S(1)} all-to-all(f16[8,48,128]{2,1,0:T(8,128)(2,1)S(1)} %convert_element_type.24), channel_id=1, replica_groups={{0,16,32,48,64,80,96,112},{8,24,40,56,72,88,104,120},{128,144,160,176,1..., dimensions={0} | all-to-all | bytes 196608 | tf_op jit(solution)/shard_map/all_to_all | solution.py:192
  91.9 16.4 %all_to_all.40 = f16[8,48,128]{2,1,0:T(8,128)(2,1)S(1)} all-to-all(f16[8,48,128]{2,1,0:T(8,128)(2,1)S(1)} %broadcast_in_dim.14), channel_id=1, replica_groups={{0,16,32,48,64,80,96,112},{8,24,40,56,72,88,104,120},{128,144,160,176,1..., dimensions={0} | all-to-all | bytes 196608 | tf_op jit(solution)/shard_map/all_to_all | solution.py:195
  108.4 1.0 broadcast_in_dim.32
  109.4 3.5 %all-to-all-start.6 = ((f16[8,48,1024]{2,1,0:T(8,128)(2,1)}), f16[8,48,1024]{2,1,0:T(8,128)(2,1)S(1)}, u32[]{:S(2)}, u32[]{:S(2)}) async-start(f16[8,48,1024]{2,1,0:T(8,128)(2,1)} %broadcast_in_dim.32), calls=%async_computation.6 | async-start | bytes 1572864 | tf_op jit(solution)/shard_map/all_to_all | solution.py:198
  112.9 0.0 copy-start.1
  112.9 0.6 fusion
  114.8 8.2 %all-to-all-done.6 = f16[8,48,1024]{2,1,0:T(8,128)(2,1)S(1)} async-done(((f16[8,48,1024]{2,1,0:T(8,128)(2,1)}), f16[8,48,1024]{2,1,0:T(8,128)(2,1)S(1)}, u32[]{:S(2)}, u32[]{:S(2)}) %all-to-all-start.6) | async-done | bytes 786464 | tf_op jit(solution)/shard_map/all_to_all | solution.py:198
  123.0 0.2 convert_multiply_fusion
  123.2 0.0 copy-done.1
  123.2 1.5 %bitcast_multiply_fusion = f32[384,1024]{1,0:T(8,128)} fusion(f32[8,48,1024]{2,1,0:T(8,128)S(1)} %convert_multiply_fusion, s32[384,1024]{1,0:T(8,128)S(1)} %copy-done.1), kind=kLoop, calls=%fused_computation | loop fusion | flops 786432 | bytes 4718592 | tf_op jit(solution)/shard_map/mul | solution.py:201
  (9 shorter events, 0.1 us)
Async XLA Ops:
  0.6 1.4 %copy-start = (s32[384,1024]{1,0:T(8,128)S(1)}, s32[384,1024]{1,0:T(8,128)}, u32[]{:S(2)}) copy-start(s32[384,1024]{1,0:T(8,128)} %flip_ref.1) | copy-start | bytes 4718596
  2.0 1.4 %copy-start.2 = (f32[1,384,1024]{2,1,0:T(8,128)S(1)}, f32[1,384,1024]{2,1,0:T(8,128)}, u32[]{:S(2)}) copy-start(f32[1,384,1024]{2,1,0:T(8,128)} %param.5) | copy-start | bytes 4718596
  3.4 0.9 copy-start.3
  4.4 48.9 %copy-start.5 = (s32[16]{0:T(128)S(1)}, s32[16]{0:T(128)}, u32[]{:S(2)}) copy-start(s32[16]{0:T(128)} %levels_ref.1) | copy-start | bytes 196
  53.2 21.0 %copy-start.4 = (bf16[256,256]{1,0:T(8,128)(2,1)S(1)}, bf16[256,256]{1,0:T(8,128)(2,1)}, u32[]{:S(2)}) copy-start(bf16[256,256]{1,0:T(8,128)(2,1)} %constant.13.clone.matrix_ref) | copy-start | bytes 393220
  109.4 13.6 %all-to-all-start.6 = ((f16[8,48,1024]{2,1,0:T(8,128)(2,1)}), f16[8,48,1024]{2,1,0:T(8,128)(2,1)S(1)}, u32[]{:S(2)}, u32[]{:S(2)}) async-start(f16[8,48,1024]{2,1,0:T(8,128)(2,1)} %broadcast_in_dim.32), calls=%async_computation.6 | async-start | bytes 1572864 | tf_op jit(solution)/shard_map/all_to_all | solution.py:198
  112.9 10.2 %copy-start.1 = (s32[384,1024]{1,0:T(8,128)S(1)}, s32[384,1024]{1,0:T(8,128)}, u32[]{:S(2)}) copy-start(s32[384,1024]{1,0:T(8,128)} %flip_ref.1) | copy-start | bytes 4718596

commit v2 on v1

v2 whole, which is shorter than its diff:
```python
import functools
import math

import jax
import jax.numpy as jnp
from jax import lax
from jax.experimental import pallas as pl
from jax.experimental.pallas import tpu as pltpu
from jax.sharding import PartitionSpec as P

F32, BF16, F16 = jnp.float32, jnp.bfloat16, jnp.float16
FOLD = 256
LANES = 128
VMEM_BYTES = 32 * 1024 * 1024
ROTATE_BYTES = 52 * 1024 * 1024
LOG2E = math.log2(math.e)


def hadamard(width):
    row = lax.broadcasted_iota(jnp.int32, (width, width), 0)
    col = lax.broadcasted_iota(jnp.int32, (width, width), 1)
    common = row & col
    step = 1
    while step < width.bit_length():
        common = common ^ (common >> step)
        step *= 2
    return (1 - 2 * (common & 1)).astype(F32).astype(BF16)


def turn(values, matrix, scale):
    count = values.shape[1] // FOLD
    parts = [values[:, k * FOLD : (k + 1) * FOLD] for k in range(count)]
    step = 1
    while step < count:
        nxt = list(parts)
        for k in range(count):
            if not k & step:
                nxt[k] = parts[k] + parts[k + step]
                nxt[k + step] = parts[k] - parts[k + step]
        parts = nxt
        step *= 2
    turned = []
    for part in parts:
        part = part * scale
        high = part.astype(BF16)
        rest = part - high.astype(F32)
        middle = rest.astype(BF16)
        low = (rest - middle.astype(F32)).astype(BF16)
        dot = functools.partial(jnp.dot, preferred_element_type=F32)
        turned.append(dot(high, matrix) + (dot(middle, matrix) + dot(low, matrix)))
    return turned


def rotate_kernel(
    grad_hbm, flip_hbm, resid_hbm, rot_ref, peak_ref, matrix_ref,
    grad, flip, resid, sems,
):
    rows, width = rot_ref.shape
    chunks = sems.shape[0]
    deep = rows // chunks
    copies = []
    for c in range(chunks):
        at = pl.ds(c * deep, deep)
        copies.append([])
        for k, (src, dst) in enumerate(((grad_hbm, grad), (flip_hbm, flip), (resid_hbm, resid))):
            copies[c].append(pltpu.make_async_copy(src.at[at], dst.at[at], sems.at[c, k]))
            copies[c][k].start()

    matrix_ref[...] = hadamard(FOLD)

    top = jnp.zeros((8, LANES), F32)
    for c in range(chunks):
        for copy in copies[c]:
            copy.wait()
        at = slice(c * deep, (c + 1) * deep)
        signed = grad[at, :] * flip[at, :].astype(F32)
        for k, part in enumerate(turn(signed, matrix_ref[...], 1.0 / math.sqrt(width))):
            cols = slice(k * FOLD, (k + 1) * FOLD)
            rotated = part + resid[at, cols]
            rot_ref[at, cols] = rotated
            size = jnp.abs(rotated)
            for lane in range(0, FOLD, LANES):
                tiles = size[:, lane : lane + LANES].reshape(-1, 8, LANES)
                top = jnp.maximum(top, jnp.max(tiles, axis=0))
    peak_ref[...] = jnp.broadcast_to(jnp.max(top, axis=0, keepdims=True), peak_ref.shape)


def table_kernel(level_ref, centre_ref, lift_ref):
    count = level_ref.shape[0]
    bottom = level_ref[0].astype(F32)
    upper = level_ref[count - 1].astype(F32)
    middle = (bottom + upper) * 0.5
    for k in range(count):
        centred = jnp.full((8, LANES), level_ref[k].astype(F32) - middle, F32)
        centre_ref[k] = centred
        lift_ref[k] = centred * centred * (-LOG2E / 72.0)


def quantize_kernel(replicas, peaks_ref, rot_ref, centre_ref, lift_ref, code_ref, full_ref, scale_ref, factor_ref):
    count = centre_ref.shape[0]
    rows, width = rot_ref.shape
    top = jnp.max(peaks_ref[...], axis=0, keepdims=True)
    peak = jnp.max(top, axis=1, keepdims=True) + 1e-06
    peak = jnp.broadcast_to(peak, (8, LANES))
    half_span = (centre_ref[count - 1] - centre_ref[0]) * 0.5
    scale = peak / half_span
    scale_ref[...] = scale
    factor_ref[...] = jnp.tile(scale[0:1] * (8.0 / replicas), (1, width // LANES))
    reach = half_span / peak * (LOG2E / 36.0)
    groups = [(r, slice(l * LANES, (l + 1) * LANES)) for l in range(width // LANES) for r in range(2)]

    def chunk(step, carry):
        row = pl.multiple_of(step * 16, 16)
        place = [rot_ref[pl.ds(row + 8 * r, 8), l] * reach for r, l in groups]
        numer, denom = [None] * len(groups), [None] * len(groups)
        for k in range(count):
            centred, lift = centre_ref[k], lift_ref[k]
            for i in range(len(groups)):
                weight = jnp.exp2(place[i] * centred + lift)
                moment = weight * centred
                numer[i] = moment if k == 0 else numer[i] + moment
                denom[i] = weight if k == 0 else denom[i] + weight
        for i in range(0, len(groups), 2):
            code = jnp.concatenate([numer[i] / denom[i], numer[i + 1] / denom[i + 1]], axis=0)
            full_ref[pl.ds(row, 16), groups[i][1]] = code
            code_ref[pl.ds(row, 16), groups[i][1]] = code.astype(BF16)
        return carry

    lax.fori_loop(0, rows // 16, chunk, 0)


def residual_kernel(rot_ref, full_ref, scale_ref, out_ref):
    scale = scale_ref[0:1, 0:1]
    out_ref[...] = rot_ref[...] - full_ref[...] * scale


def partial_kernel(codes_ref, matrix_ref, out_ref):
    width = codes_ref.shape[2]
    total = codes_ref[0].astype(F32)
    for k in range(1, codes_ref.shape[0]):
        total = total + codes_ref[k].astype(F32)
    turned = turn(total, matrix_ref[...], 1.0 / math.sqrt(width))
    for k, part in enumerate(turned):
        for at in range(0, FOLD, LANES):
            out_ref[(k * FOLD + at) // LANES] = part[:, at : at + LANES]


def grouped(pieces, axes, groups):
    return lax.all_to_all(pieces, axes, 0, 0, axis_index_groups=groups)


def on_device(gradient, residual, sign_flips, level_table):
    _, rows, width = gradient.shape
    levels = level_table.shape[0]
    replicas, splits = lax.axis_size("dp"), lax.axis_size("fsdp")
    depth = 16
    ys, pairs = range(replicas // depth), range(depth // 2)
    near = [[y * depth + 2 * h + l for y in ys for l in range(2)] for h in pairs]
    far = [[y * depth + 2 * h + l for h in pairs] for y in ys for l in range(2)]
    line = [[y * depth + z for z in range(depth)] for y in ys]
    plane = [[(y * depth + z) * splits + f for y in ys for f in range(splits)] for z in range(depth)]
    params = functools.partial(pltpu.CompilerParams, vmem_limit_bytes=VMEM_BYTES)
    hbm, vmem = pl.BlockSpec(memory_space=pltpu.HBM), pl.BlockSpec(memory_space=pltpu.VMEM)
    like = jax.ShapeDtypeStruct

    chunks = 4
    rotated, peaks, matrix = pl.pallas_call(
        rotate_kernel,
        in_specs=[hbm] * 3,
        out_specs=[vmem] * 3,
        out_shape=[
            like((rows, width), F32),
            like((len(plane[0]), LANES), F32),
            like((FOLD, FOLD), BF16),
        ],
        scratch_shapes=[
            pltpu.VMEM((rows, width), F32),
            pltpu.VMEM((rows, width), jnp.int32),
            pltpu.VMEM((rows, width), F32),
            pltpu.SemaphoreType.DMA((chunks, 3)),
        ],
        compiler_params=pltpu.CompilerParams(vmem_limit_bytes=ROTATE_BYTES),
        name="rotate",
    )(gradient[0], sign_flips, residual[0])
    centred, lift = pl.pallas_call(
        table_kernel,
        in_specs=[pl.BlockSpec(memory_space=pltpu.SMEM)],
        out_specs=[vmem] * 2,
        out_shape=[like((levels, 8, LANES), F32)] * 2,
        compiler_params=params(),
        name="table",
    )(level_table)

    peaks = grouped(peaks, ("dp", "fsdp"), plane)
    peaks = jnp.broadcast_to(jnp.max(peaks, axis=0, keepdims=True), (depth, LANES))
    peaks = grouped(peaks, "dp", line)

    codes, full, scale, factor = pl.pallas_call(
        functools.partial(quantize_kernel, replicas),
        in_specs=[vmem] * 4,
        out_specs=[vmem] * 4,
        out_shape=[
            like((rows, width), BF16),
            like((rows, width), F32),
            like((8, LANES), F32),
            like((1, width), F32),
        ],
        compiler_params=params(),
        name="quantize",
    )(peaks, rotated, centred, lift)

    block = 96
    tile = pl.BlockSpec((block, width), lambda i: (i, 0))
    new_residual = pl.pallas_call(
        residual_kernel,
        grid=(rows // block,),
        in_specs=[tile, tile, pl.BlockSpec((8, LANES), lambda i: (0, 0))],
        out_specs=tile,
        out_shape=like((rows, width), F32),
        compiler_params=params(),
        cost_estimate=pl.CostEstimate(flops=2 * rows * width, bytes_accessed=12 * rows * width, transcendentals=0),
        name="residual",
    )(rotated, full, scale)

    first, second = len(near[0]), len(far[0])
    share = rows // first
    codes = grouped(codes.reshape(first, share, width), "dp", near)
    partial = pl.pallas_call(
        partial_kernel,
        out_shape=like((second, share, width // second), F32),
        compiler_params=params(),
        name="partial",
    )(codes, matrix)
    partial = grouped(partial.astype(F16), "dp", far)
    mean = jnp.sum(partial.astype(F32), axis=0) * 0.125
    mean = jnp.broadcast_to(mean.astype(F16)[None], partial.shape)
    mean = grouped(mean, "dp", far)
    mean = mean.transpose(1, 0, 2).reshape(share, width)
    mean = grouped(jnp.broadcast_to(mean[None], (first, share, width)), "dp", near)
    mean = mean.reshape(rows, width).astype(F32) * factor * sign_flips.astype(F32)
    return mean, new_residual[None]


def solution(mesh):
    placed = (P("dp", "fsdp", None), P("dp", "fsdp", None), P("fsdp", None), P())
    return jax.shard_map(
        on_device,
        mesh=mesh,
        in_specs=placed,
        out_specs=(P("fsdp", None), P("dp", "fsdp", None)),
        check_vma=False,
    )
```

time: 126 us -> 117 us (0.929)
  blocking collectives: 91.9 us -> 60.6 us
  starting transfers between devices: 3.55 us -> 18.2 us
  waiting for transfers between devices: 8.16 us -> 20.1 us
  local copies, waits for them, and re-layouts: 5.37 us -> 1.63 us
  other arithmetic: 1.7 us -> 3.22 us
  between operations: 2 us -> 0.72 us
    all_to_all x6 -> x4, blocking collectives: 91.9 us -> 60.6 us  [grouped(): return lax.all_to_all(pieces, axes, 0, 0, axis_index_groups=groups)]
    all_to_all x1 -> x2, starting transfers between devices: 3.55 us -> 18.2 us  [grouped(): return lax.all_to_all(pieces, axes, 0, 0, axis_index_groups=groups)]
    all_to_all x1 -> x2, waiting for transfers between devices: 8.16 us -> 20.1 us  [grouped(): return lax.all_to_all(pieces, axes, 0, 0, axis_index_groups=groups)]
    unnamed x12 -> x2, local copies, waits for them, and re-layouts: 3.73 us -> 0.01 us
    mul x2 -> x1, other arithmetic: 1.62 us -> 3.1 us  [on_device(): mean.reshape(rows, width).astype(F32) * factor * sign_flips.astype(F32)]
    pallas_call x3 -> x5, Pallas kernels: 12 us -> 11.4 us  [the longest x1 5.5 us: on_device(): pl.pallas_call(functools.partial(quantize_kernel, replicas), in_specs=[vm...]
  transfers between devices with their start and end apart: 1 -> 2, of which waited for: 1 -> 2; matrix products, arithmetic and copies ran while one was open for 0% -> 0% of each run, Pallas kernels for 0% -> 2%
where the time goes in v2:
time: 117 us; the launch traced here: 116 us
  blocking collectives  60.6 us (52%)
  waiting for transfers between devices  20.1 us (17%)
  starting transfers between devices  18.2 us (16%)
  Pallas kernels  11.4 us (10%)
  other arithmetic  3.22 us (3%)
  local copies, waits for them, and re-layouts  1.63 us (1%)
    all_to_all x4, blocking collectives, grouped(): return lax.all_to_all(pieces, axes, 0, 0, axis_index_groups=groups)  60.6 us
    all_to_all x2, waiting for transfers between devices, grouped(): return lax.all_to_all(pieces, axes, 0, 0, axis_index_groups=groups)  20.1 us
    all_to_all x2, starting transfers between devices, grouped(): return lax.all_to_all(pieces, axes, 0, 0, axis_index_groups=groups)  18.2 us
    pallas_call x1, Pallas kernels, on_device(): pl.pallas_call(functools.partial(quantize_kernel, replicas), in_specs=[vm...  5.5 us
    mul x1, other arithmetic, on_device(): mean.reshape(rows, width).astype(F32) * factor * sign_flips.astype(F32)  3.1 us
    pallas_call x1, Pallas kernels, on_device(): pl.pallas_call(rotate_kernel, in_specs=[hbm] * 3, out_specs=[vmem] * 3, o...  3.09 us
  transfers between devices with their start and end apart: 2, of which 2 were waited for; matrix products, arithmetic and copies ran while one was open for 0% of the time, Pallas kernels for 2%

profile of v2, /device:TPU:6, one launch (start us, length us, event | category | flops | bytes accessed | tf_op | source)
XLA Modules:
  0.0 115.8 jit_solution(9527737771295459469)
XLA Ops:
  0.6 0.0 copy-start
  0.6 3.1 %rotate.1 = (f32[384,1024]{1,0:T(8,128)S(1)}, f32[32,128]{1,0:T(8,128)S(1)}, bf16[256,256]{1,0:T(8,128)(2,1)S(1)}) custom-call(f32[384,1024]{1,0:T(8,128)} %bitcast.22, s32[384,1024]{1,0:T(8,128)} %flip_hbm.1, f32[384,1024]{1,0:T(8,128)} %bitcast.23), custom_call_target="tpu_custom_call" | custom-call | tf_op jit(solution)/shard_map/rotate/pallas_call | solution.py:167
  3.7 14.1 %all_to_all.37 = f32[32,1,128]{2,1,0:T(1,128)S(1)} all-to-all(f32[32,1,128]{2,1,0:T(1,128)S(1)} %bitcast.20), channel_id=1, replica_groups={{0,1,2,3,4,5,6,7,128,129,130,131,132,133,134,135,256,257,258,259,260,26..., dimensions={0} | all-to-all | bytes 32768 | tf_op jit(solution)/shard_map/all_to_all | solution.py:149
  17.8 0.1 reduce_max.9
  17.9 0.6 broadcast_in_dim.10
  18.5 14.0 %all-to-all-start.1 = ((f32[16,1,128]{2,1,0:T(1,128)}), f32[16,1,128]{2,1,0:T(1,128)S(1)}, u32[]{:S(2)}, u32[]{:S(2)}) async-start(f32[16,1,128]{2,1,0:T(1,128)} %broadcast_in_dim.10), calls=%async_computation.1 | async-start | bytes 16384 | tf_op jit(solution)/shard_map/all_to_all | solution.py:149
  32.5 0.0 copy-done
  32.5 0.6 table.1
  33.1 11.8 %all-to-all-done.1 = f32[16,1,128]{2,1,0:T(1,128)S(1)} async-done(((f32[16,1,128]{2,1,0:T(1,128)}), f32[16,1,128]{2,1,0:T(1,128)S(1)}, u32[]{:S(2)}, u32[]{:S(2)}) %all-to-all-start.1) | async-done | bytes 8224 | tf_op jit(solution)/shard_map/all_to_all | solution.py:149
  44.8 5.5 %quantize.1 = (bf16[384,1024]{1,0:T(8,128)(2,1)S(1)}, f32[384,1024]{1,0:T(8,128)S(1)}, f32[8,128]{1,0:T(8,128)S(1)}, f32[1,1024]{1,0:T(1,128)S(1)}) custom-call(f32[16,128]{1,0:T(8,128)S(1)} %bitcast.19, f32[384,1024]{1,0:T(8,128)S(1)} %get-tuple-element.12.rot_ref, f32[16,8,128]{2,1,0:T(8,128)S(1)} %get-tuple-element.13.centre_ref, ...), custom_call_target="tpu_custom_call" | custom-call | tf_op jit(solution)/shard_map/quantize/pallas_call | solution.py:198
  50.4 14.2 %all_to_all.38.codes_ref = bf16[8,48,1024]{2,1,0:T(8,128)(2,1)S(1)} all-to-all(bf16[8,48,1024]{2,1,0:T(8,128)(2,1)S(1)} %bitcast.18), channel_id=1, replica_groups={{0,8,128,136,256,264,384,392},{16,24,144,152,272,280,400,408},{32,40,16..., dimensions={0} | all-to-all | bytes 1572864 | tf_op jit(solution)/shard_map/all_to_all | solution.py:149
  64.6 0.4 partial.1
  65.1 16.1 %all_to_all.39 = f16[8,48,128]{2,1,0:T(8,128)(2,1)S(1)} all-to-all(f16[8,48,128]{2,1,0:T(8,128)(2,1)S(1)} %convert_element_type.22), channel_id=1, replica_groups={{0,16,32,48,64,80,96,112},{8,24,40,56,72,88,104,120},{128,144,160,176,1..., dimensions={0} | all-to-all | bytes 196608 | tf_op jit(solution)/shard_map/all_to_all | solution.py:149
  81.2 16.1 %all_to_all.40 = f16[8,48,128]{2,1,0:T(8,128)(2,1)S(1)} all-to-all(f16[8,48,128]{2,1,0:T(8,128)(2,1)S(1)} %broadcast_in_dim.11), channel_id=1, replica_groups={{0,16,32,48,64,80,96,112},{8,24,40,56,72,88,104,120},{128,144,160,176,1..., dimensions={0} | all-to-all | bytes 196608 | tf_op jit(solution)/shard_map/all_to_all | solution.py:149
  97.4 1.0 broadcast_in_dim.25
  98.4 4.2 %all-to-all-start.5 = ((f16[8,48,1024]{2,1,0:T(8,128)(2,1)}), f16[8,48,1024]{2,1,0:T(8,128)(2,1)}, u32[]{:S(2)}, u32[]{:S(2)}) async-start(f16[8,48,1024]{2,1,0:T(8,128)(2,1)} %broadcast_in_dim.25), calls=%async_computation.5 | async-start | bytes 1572864 | tf_op jit(solution)/shard_map/all_to_all | solution.py:149
  102.6 1.8 %residual.1 = f32[384,1024]{1,0:T(8,128)} custom-call(f32[384,1024]{1,0:T(8,128)S(1)} %get-tuple-element.12.rot_ref, f32[384,1024]{1,0:T(8,128)S(1)} %get-tuple-element.18.full_ref, f32[8,128]{1,0:T(8,128)S(1)} %get-tuple-element.19.scale_ref), custom_call_target="tpu_custom_call" | custom-call | flops 786432 | bytes 4718592 | tf_op jit(solution)/shard_map/residual/pallas_call | solution.py:214
  104.4 8.3 %all-to-all-done.5 = f16[8,48,1024]{2,1,0:T(8,128)(2,1)} async-done(((f16[8,48,1024]{2,1,0:T(8,128)(2,1)}), f16[8,48,1024]{2,1,0:T(8,128)(2,1)}, u32[]{:S(2)}, u32[]{:S(2)}) %all-to-all-start.5) | async-done | bytes 786464 | tf_op jit(solution)/shard_map/all_to_all | solution.py:149
  112.7 3.1 %fusion = f32[384,1024]{1,0:T(8,128)} fusion(s32[384,1024]{1,0:T(8,128)} %flip_hbm.1, f16[8,48,1024]{2,1,0:T(8,128)(2,1)} %all-to-all-done.5, f32[1024]{0:T(1024)S(1)} %bitcast.21), kind=kLoop, calls=%fused_computation.1 | loop fusion | flops 1572864 | bytes 3936256 | tf_op jit(solution)/shard_map/mul | solution.py:240
  (5 shorter events, 0.1 us)
Async XLA Ops:
  0.6 31.9 %copy-start = (s32[16]{0:T(128)S(1)}, s32[16]{0:T(128)}, u32[]{:S(2)}) copy-start(s32[16]{0:T(128)} %level_ref.1) | copy-start | bytes 196
  18.5 26.3 %all-to-all-start.1 = ((f32[16,1,128]{2,1,0:T(1,128)}), f32[16,1,128]{2,1,0:T(1,128)S(1)}, u32[]{:S(2)}, u32[]{:S(2)}) async-start(f32[16,1,128]{2,1,0:T(1,128)} %broadcast_in_dim.10), calls=%async_computation.1 | async-start | bytes 16384 | tf_op jit(solution)/shard_map/all_to_all | solution.py:149
  98.4 14.4 %all-to-all-start.5 = ((f16[8,48,1024]{2,1,0:T(8,128)(2,1)}), f16[8,48,1024]{2,1,0:T(8,128)(2,1)}, u32[]{:S(2)}, u32[]{:S(2)}) async-start(f16[8,48,1024]{2,1,0:T(8,128)(2,1)} %broadcast_in_dim.25), calls=%async_computation.5 | async-start | bytes 1572864 | tf_op jit(solution)/shard_map/all_to_all | solution.py:149

commit v3 on v2

v3 whole, which is shorter than its diff:
```python
import functools
import math

import jax
import jax.numpy as jnp
from jax import lax
from jax.experimental import pallas as pl
from jax.experimental.pallas import tpu as pltpu
from jax.sharding import PartitionSpec as P

F32, BF16, F16 = jnp.float32, jnp.bfloat16, jnp.float16
FOLD = 256
LANES = 128
VMEM_BYTES = 32 * 1024 * 1024
ROTATE_BYTES = 52 * 1024 * 1024
LOG2E = math.log2(math.e)


def hadamard(width):
    row = lax.broadcasted_iota(jnp.int32, (width, width), 0)
    col = lax.broadcasted_iota(jnp.int32, (width, width), 1)
    common = row & col
    step = 1
    while step < width.bit_length():
        common = common ^ (common >> step)
        step *= 2
    return (1 - 2 * (common & 1)).astype(F32).astype(BF16)


def turn(values, matrix, scale):
    count = values.shape[1] // FOLD
    parts = [values[:, k * FOLD : (k + 1) * FOLD] for k in range(count)]
    step = 1
    while step < count:
        nxt = list(parts)
        for k in range(count):
            if not k & step:
                nxt[k] = parts[k] + parts[k + step]
                nxt[k + step] = parts[k] - parts[k + step]
        parts = nxt
        step *= 2
    turned = []
    for part in parts:
        part = part * scale
        high = part.astype(BF16)
        rest = part - high.astype(F32)
        middle = rest.astype(BF16)
        low = (rest - middle.astype(F32)).astype(BF16)
        dot = functools.partial(jnp.dot, preferred_element_type=F32)
        turned.append(dot(high, matrix) + (dot(middle, matrix) + dot(low, matrix)))
    return turned


def rotate_kernel(
    depth, grad_hbm, flip_hbm, resid_hbm, own_ref, next_ref, across_ref, last_ref, peak_ref, matrix_ref,
    grad, flip, resid, sems,
):
    outs = (own_ref, next_ref, across_ref, last_ref)
    ys = len(outs)
    deep, width = own_ref.shape
    here = lax.div(lax.axis_index("dp"), depth)
    order = (1, 2, 3, 0)
    copies = {}
    for k in order:
        chunk = lax.rem(here + k, ys)
        source, target = pl.ds(pl.multiple_of(chunk * deep, 8), deep), pl.ds(k * deep, deep)
        copies[k] = [
            pltpu.make_async_copy(src.at[source], dst.at[target], sems.at[k, i])
            for i, (src, dst) in enumerate(((grad_hbm, grad), (flip_hbm, flip), (resid_hbm, resid)))
        ]
        for copy in copies[k]:
            copy.start()
    matrix_ref[...] = hadamard(FOLD)

    top = jnp.zeros((8, LANES), F32)
    for k in order:
        for copy in copies[k]:
            copy.wait()
        at = slice(k * deep, (k + 1) * deep)
        signed = grad[at, :] * flip[at, :].astype(F32)
        for j, part in enumerate(turn(signed, matrix_ref[...], 1.0 / math.sqrt(width))):
            cols = slice(j * FOLD, (j + 1) * FOLD)
            rotated = part + resid[at, cols]
            outs[k][:, cols] = rotated
            size = jnp.abs(rotated)
            for lane in range(0, FOLD, LANES):
                tiles = size[:, lane : lane + LANES].reshape(-1, 8, LANES)
                top = jnp.maximum(top, jnp.max(tiles, axis=0))
    peak_ref[...] = jnp.broadcast_to(jnp.max(top, axis=0, keepdims=True), peak_ref.shape)


def table_kernel(level_ref, centre_ref, lift_ref):
    count = level_ref.shape[0]
    bottom = level_ref[0].astype(F32)
    upper = level_ref[count - 1].astype(F32)
    middle = (bottom + upper) * 0.5
    for k in range(count):
        centred = jnp.full((8, LANES), level_ref[k].astype(F32) - middle, F32)
        centre_ref[k] = centred
        lift_ref[k] = centred * centred * (-LOG2E / 72.0)


def soft_codes(rows, cols, load, reach, centre_ref, lift_ref):
    place = [load(r, l) * reach for l in cols for r in rows]
    numer, denom = [None] * len(place), [None] * len(place)
    for k in range(centre_ref.shape[0]):
        centred, lift = centre_ref[k], lift_ref[k]
        for i in range(len(place)):
            weight = jnp.exp2(place[i] * centred + lift)
            moment = weight * centred
            numer[i] = moment if k == 0 else numer[i] + moment
            denom[i] = weight if k == 0 else denom[i] + weight
    return [n / d for n, d in zip(numer, denom)]


def scales(peaks_ref, centre_ref):
    top = jnp.max(peaks_ref[...], axis=0, keepdims=True)
    peak = jnp.max(top, axis=1, keepdims=True) + 1e-06
    peak = jnp.broadcast_to(peak, (8, LANES))
    half_span = (centre_ref[centre_ref.shape[0] - 1] - centre_ref[0]) * 0.5
    return peak / half_span, half_span / peak * (LOG2E / 36.0)


def partial_kernel(
    replicas, peaks_ref, p0, p1, p2, p3, centre_ref, lift_ref, matrix_ref, out_ref, factor_ref, total_ref
):
    scale, reach = scales(peaks_ref, centre_ref)
    pieces = (p0, p1, p2, p3)
    rows, width = p0.shape
    factor_ref[...] = jnp.tile(scale[0:1] * (8.0 / replicas), (1, width // LANES))
    wide = 4 * LANES
    per_row = width // wide

    def chunk(step, carry):
        row = pl.multiple_of((step // per_row) * 8, 8)
        col = pl.multiple_of((step % per_row) * wide, wide)

        def at(l):
            return pl.ds(row, 8), pl.ds(col + l * LANES, LANES)

        codes = soft_codes(pieces, range(4), lambda piece, l: piece[at(l)], reach, centre_ref, lift_ref)
        for l in range(4):
            total = None
            for code in codes[l * 4 : (l + 1) * 4]:
                code = code.astype(BF16).astype(F32)
                total = code if total is None else total + code
            total_ref[at(l)] = total
        return carry

    lax.fori_loop(0, (rows // 8) * per_row, chunk, 0, unroll=2)
    turned = turn(total_ref[...], matrix_ref[...], 1.0 / math.sqrt(width))
    half = rows // 2
    for k, part in enumerate(turned):
        for at in range(0, FOLD, LANES):
            for low in range(2):
                piece = (k * FOLD + at) // LANES * 2 + low
                out_ref[piece] = part[low * half : (low + 1) * half, at : at + LANES]


def residual_kernel(depth, peaks_ref, r0, r1, r2, r3, centre_ref, lift_ref, out_hbm, out, sems):
    scale, reach = scales(peaks_ref, centre_ref)
    deep, width = r0.shape
    here = lax.div(lax.axis_index("dp"), depth)
    copies = []
    for c, rot_ref in enumerate((r0, r1, r2, r3)):

        def chunk(step, carry, c=c, rot_ref=rot_ref):
            row = pl.multiple_of(step * 16, 16)

            def at(r, l):
                return pl.ds(row + 8 * r, 8), slice(l * LANES, (l + 1) * LANES)

            tiles = [(r, l) for l in range(width // LANES) for r in range(2)]
            codes = soft_codes(
                range(2), range(width // LANES), lambda r, l: rot_ref[at(r, l)], reach, centre_ref, lift_ref
            )
            for (r, l), code in zip(tiles, codes):
                out[(c,) + at(r, l)] = rot_ref[at(r, l)] - code * scale
            return carry

        lax.fori_loop(0, deep // 16, chunk, 0, unroll=2)
        target = pl.ds(pl.multiple_of(lax.rem(here + c, 4) * deep, 8), deep)
        copies.append(pltpu.make_async_copy(out.at[c], out_hbm.at[target], sems.at[c]))
        copies[c].start()
    for copy in copies:
        copy.wait()


def grouped(pieces, axes, groups):
    return lax.all_to_all(pieces, axes, 0, 0, axis_index_groups=groups)


def on_device(gradient, residual, sign_flips, level_table):
    _, rows, width = gradient.shape
    levels = level_table.shape[0]
    replicas, splits = lax.axis_size("dp"), lax.axis_size("fsdp")
    depth = 16
    ys, pairs = range(replicas // depth), range(depth // 2)
    near = [[y * depth + 2 * h + l for y in ys for l in range(2)] for h in pairs]
    far = [[y * depth + 2 * h + l for h in pairs] for y in ys for l in range(2)]
    line = [[y * depth + z for z in range(depth)] for y in ys]
    plane = [[(y * depth + z) * splits + f for y in ys for f in range(splits)] for z in range(depth)]
    params = functools.partial(pltpu.CompilerParams, vmem_limit_bytes=VMEM_BYTES)
    hbm, vmem = pl.BlockSpec(memory_space=pltpu.HBM), pl.BlockSpec(memory_space=pltpu.VMEM)
    like = jax.ShapeDtypeStruct

    count = len(ys)
    deep = rows // count
    *chunks, peaks, matrix = pl.pallas_call(
        functools.partial(rotate_kernel, depth),
        in_specs=[hbm] * 3,
        out_specs=[vmem] * (count + 2),
        out_shape=[like((deep, width), F32)] * count
        + [like((len(plane[0]), LANES), F32), like((FOLD, FOLD), BF16)],
        scratch_shapes=[
            pltpu.VMEM((rows, width), F32),
            pltpu.VMEM((rows, width), jnp.int32),
            pltpu.VMEM((rows, width), F32),
            pltpu.SemaphoreType.DMA((count, 3)),
        ],
        compiler_params=pltpu.CompilerParams(vmem_limit_bytes=ROTATE_BYTES),
        name="rotate",
    )(gradient[0], sign_flips, residual[0])

    def ahead(chunk, k):
        hops = [(y * depth + z, (y + k) % count * depth + z) for y in ys for z in range(depth)]
        return lax.ppermute(chunk, "dp", hops)

    pieces = [chunks[0]] + [ahead(chunks[k], k) for k in range(1, count)]
    centred, lift = pl.pallas_call(
        table_kernel,
        in_specs=[pl.BlockSpec(memory_space=pltpu.SMEM)],
        out_specs=[vmem] * 2,
        out_shape=[like((levels, 8, LANES), F32)] * 2,
        compiler_params=params(),
        name="table",
    )(level_table)

    peaks = grouped(peaks, ("dp", "fsdp"), plane)
    peaks = jnp.broadcast_to(jnp.max(peaks, axis=0, keepdims=True), (depth, LANES))
    peaks = grouped(peaks, "dp", line)

    first, second = len(near[0]), len(far[0])
    share = rows // first
    partial, factor = pl.pallas_call(
        functools.partial(partial_kernel, replicas),
        in_specs=[vmem] * 8,
        out_specs=[vmem] * 2,
        out_shape=[like((depth, share, width // second), F32), like((1, width), F32)],
        scratch_shapes=[pltpu.VMEM((deep, width), F32)],
        compiler_params=params(),
        name="partial",
    )(peaks, *pieces, centred, lift, matrix)
    new_residual = pl.pallas_call(
        functools.partial(residual_kernel, depth),
        in_specs=[vmem] * 7,
        out_specs=hbm,
        out_shape=like((rows, width), F32),
        scratch_shapes=[pltpu.VMEM((count, deep, width), F32), pltpu.SemaphoreType.DMA((count,))],
        compiler_params=params(),
        cost_estimate=pl.CostEstimate(flops=100 * rows * width, bytes_accessed=12 * rows * width, transcendentals=16 * rows * width),
        name="residual",
    )(peaks, *chunks, centred, lift)

    partial = grouped(partial.astype(F16), "dp", line)
    partial, new_residual = lax.optimization_barrier((partial, new_residual))
    mean = jnp.sum(partial.astype(F32), axis=0) * 0.125
    mean = jnp.broadcast_to(mean.astype(F16)[None], (second,) + mean.shape)
    mean = grouped(mean, "dp", far)
    mean = mean.transpose(1, 0, 2).reshape(share, width)
    mean = grouped(jnp.broadcast_to(mean[None], (first, share, width)), "dp", near)
    mean = mean.reshape(rows, width).astype(F32) * factor * sign_flips.astype(F32)
    return mean, new_residual[None]


def solution(mesh):
    placed = (P("dp", "fsdp", None), P("dp", "fsdp", None), P("fsdp", None), P())
    return jax.shard_map(
        on_device,
        mesh=mesh,
        in_specs=placed,
        out_specs=(P("fsdp", None), P("dp", "fsdp", None)),
        check_vma=False,
    )
```

time: 117 us -> 118 us (level)
  blocking collectives: 60.6 us -> 46.4 us
  starting transfers between devices: 18.2 us -> 30.3 us
  Pallas kernels: 11.4 us -> 15.6 us
  waiting for transfers between devices: 20.1 us -> 21.3 us
    all_to_all x4 -> x3, blocking collectives: 60.6 us -> 46.4 us  [grouped(): return lax.all_to_all(pieces, axes, 0, 0, axis_index_groups=groups)]
    ppermute x0 -> x3, starting transfers between devices: none -> 11.6 us  [ahead(): return lax.ppermute(chunk, 'dp', hops)]
    pallas_call x4 -> x3, Pallas kernels: 10.8 us -> 15.1 us  [the longest x1 6.2 us: on_device(): pl.pallas_call(functools.partial(residual_kernel, depth), in_specs=[vmem]...]
    mul x1, other arithmetic: 3.1 us -> 1.45 us  [on_device(): mean.reshape(rows, width).astype(F32) * factor * sign_flips.astype(F32)]
  transfers between devices with their start and end apart: 2 -> 5, of which waited for: 2 -> 2; matrix products, arithmetic and copies ran while one was open for 0% -> 1% of each run, Pallas kernels for 2% -> 6%
where the time goes in v3:
time: 118 us; the launch traced here: 117 us
  blocking collectives  46.4 us (39%)
  starting transfers between devices  30.3 us (26%)
  waiting for transfers between devices  21.3 us (18%)
  Pallas kernels  15.6 us (13%)
  other arithmetic  2.25 us (2%)
    all_to_all x3, blocking collectives, grouped(): return lax.all_to_all(pieces, axes, 0, 0, axis_index_groups=groups)  46.4 us
    all_to_all x2, waiting for transfers between devices, grouped(): return lax.all_to_all(pieces, axes, 0, 0, axis_index_groups=groups)  21.3 us
    all_to_all x2, starting transfers between devices, grouped(): return lax.all_to_all(pieces, axes, 0, 0, axis_index_groups=groups)  18.7 us
    ppermute x3, starting transfers between devices, ahead(): return lax.ppermute(chunk, 'dp', hops)  11.6 us
    pallas_call x1, Pallas kernels, on_device(): pl.pallas_call(functools.partial(residual_kernel, depth), in_specs=[vmem]...  6.2 us
    pallas_call x1, Pallas kernels, on_device(): pl.pallas_call(functools.partial(partial_kernel, replicas), in_specs=[vme...  5.8 us
    pallas_call x1, Pallas kernels, on_device(): pl.pallas_call(functools.partial(rotate_kernel, depth), in_specs=[hbm] *...  3.08 us
  transfers between devices with their start and end apart: 5, of which 2 were waited for; matrix products, arithmetic and copies ran while one was open for 1% of the time, Pallas kernels for 6%

profile of v3, /device:TPU:6, one launch (start us, length us, event | category | flops | bytes accessed | tf_op | source)
XLA Modules:
  0.0 117.3 jit_solution(1905898085080826384)
XLA Ops:
  0.6 0.0 copy-start
  0.6 3.1 %rotate.1 = (f32[96,1024]{1,0:T(8,128)S(1)}, f32[96,1024]{1,0:T(8,128)S(1)}, f32[96,1024]{1,0:T(8,128)S(1)}, f32[96,1024]{1,0:T(8,128)S(1)}, f32[32,128]{1,0:T(8,128)S(1)}, /*index=5*/bf16[256,256]{1,0:T(8,128)(2,1)S(1)}) custom-call(f32[384,1024]{1,0:T(8,128)} %bitcast.21, s32[384,1024]{1,0:T(8,128)} %flip_hbm.1, f32[384,1024]{1,0:T(8,128)} %bitcast.22), custom_call_target="tpu_custom_call" | custom-call | tf_op jit(solution)/shard_map/rotate/pallas_call | solution.py:209
  3.7 3.5 %collective-permute-start = (f32[96,1024]{1,0:T(8,128)S(1)}, f32[96,1024]{1,0:T(8,128)S(1)}, u32[]{:S(2)}, u32[]{:S(2)}) collective-permute-start(f32[96,1024]{1,0:T(8,128)S(1)} %get-tuple-element.16.r1), channel_id=1, source_target_pairs={{0,128},{8,136},{16,144},{24,152},{32,160},{40,168},{48,176},{56,1... | collective-permute-start | bytes 1179656 | tf_op jit(solution)/shard_map/ppermute | solution.py:227
  7.2 4.8 %collective-permute-start.1 = (f32[96,1024]{1,0:T(8,128)S(1)}, f32[96,1024]{1,0:T(8,128)S(1)}, u32[]{:S(2)}, u32[]{:S(2)}) collective-permute-start(f32[96,1024]{1,0:T(8,128)S(1)} %get-tuple-element.17.r2), channel_id=1, source_target_pairs={{0,256},{8,264},{16,272},{24,280},{32,288},{40,296},{48,304},{56,3... | collective-permute-start | bytes 1179656 | tf_op jit(solution)/shard_map/ppermute | solution.py:227
  12.0 3.3 %collective-permute-start.2 = (f32[96,1024]{1,0:T(8,128)S(1)}, f32[96,1024]{1,0:T(8,128)S(1)}, u32[]{:S(2)}, u32[]{:S(2)}) collective-permute-start(f32[96,1024]{1,0:T(8,128)S(1)} %get-tuple-element.18.r3), channel_id=1, source_target_pairs={{0,384},{8,392},{16,400},{24,408},{32,416},{40,424},{48,432},{56,4... | collective-permute-start | bytes 1179656 | tf_op jit(solution)/shard_map/ppermute | solution.py:227
  15.3 13.6 %all_to_all.32 = f32[32,1,128]{2,1,0:T(1,128)S(1)} all-to-all(f32[32,1,128]{2,1,0:T(1,128)S(1)} %bitcast.19), channel_id=1, replica_groups={{0,1,2,3,4,5,6,7,128,129,130,131,132,133,134,135,256,257,258,259,260,26..., dimensions={0} | all-to-all | bytes 32768 | tf_op jit(solution)/shard_map/all_to_all | solution.py:190
  28.9 0.1 reduce_max.9
  29.0 0.6 broadcast_in_dim.10
  29.6 15.2 %all-to-all-start.1 = ((f32[16,1,128]{2,1,0:T(1,128)}), f32[16,1,128]{2,1,0:T(1,128)S(1)}, u32[]{:S(2)}, u32[]{:S(2)}) async-start(f32[16,1,128]{2,1,0:T(1,128)} %broadcast_in_dim.10), calls=%async_computation.1 | async-start | bytes 16384 | tf_op jit(solution)/shard_map/all_to_all | solution.py:190
  44.8 0.0 copy-done
  44.8 0.6 table.1
  45.4 11.8 %all-to-all-done.1 = f32[16,1,128]{2,1,0:T(1,128)S(1)} async-done(((f32[16,1,128]{2,1,0:T(1,128)}), f32[16,1,128]{2,1,0:T(1,128)S(1)}, u32[]{:S(2)}, u32[]{:S(2)}) %all-to-all-start.1) | async-done | bytes 8224 | tf_op jit(solution)/shard_map/all_to_all | solution.py:190
  57.2 0.0 collective-permute-done.p1
  57.2 0.0 collective-permute-done.1.p2
  57.2 0.0 collective-permute-done.2.p3
  57.2 5.8 %partial.1 = (f32[16,48,128]{2,1,0:T(8,128)S(1)}, f32[1,1024]{1,0:T(1,128)S(1)}) custom-call(f32[16,128]{1,0:T(8,128)S(1)} %bitcast.17, f32[96,1024]{1,0:T(8,128)S(1)} %get-tuple-element.15.p0.r0, f32[96,1024]{1,0:T(8,128)S(1)} %collective-permute-done.p1, f32[96,1024]{1,0:T(8,128)S(1)} %collective-permute-done.1.p2, ...), custom_call_target="tpu_custom_call" | custom-call | tf_op jit(solution)/shard_map/partial/pallas_call | solution.py:245
  63.0 0.7 convert_element_type.22
  63.7 3.5 %all-to-all-start.2 = ((f16[16,48,128]{2,1,0:T(8,128)(2,1)}), f16[16,48,128]{2,1,0:T(8,128)(2,1)S(1)}, u32[]{:S(2)}, u32[]{:S(2)}) async-start(f16[16,48,128]{2,1,0:T(8,128)(2,1)} %convert_element_type.22), calls=%async_computation.2 | async-start | bytes 393216 | tf_op jit(solution)/shard_map/all_to_all | solution.py:190
  67.2 6.2 %residual.1 = f32[384,1024]{1,0:T(8,128)} custom-call(f32[16,128]{1,0:T(8,128)S(1)} %bitcast.18, f32[96,1024]{1,0:T(8,128)S(1)} %get-tuple-element.15.p0.r0, f32[96,1024]{1,0:T(8,128)S(1)} %get-tuple-element.16.r1, f32[96,1024]{1,0:T(8,128)S(1)} %get-tuple-element.17.r2, f32[96,1024]{1,0:T(8,128)S(1)} %get-tuple-element.18.r3, ...), custom_call_target="tpu_custom_call" | custom-call | flops 39321600 | bytes 4718592 | tf_op jit(solution)/shard_map/residual/pallas_call | solution.py:254
  73.4 0.0 copy-start.1
  73.4 9.5 %all-to-all-done.2 = f16[16,48,128]{2,1,0:T(8,128)(2,1)S(1)} async-done(((f16[16,48,128]{2,1,0:T(8,128)(2,1)}), f16[16,48,128]{2,1,0:T(8,128)(2,1)S(1)}, u32[]{:S(2)}, u32[]{:S(2)}) %all-to-all-start.2) | async-done | bytes 196640 | tf_op jit(solution)/shard_map/all_to_all | solution.py:190
  83.0 18.3 %all_to_all.33 = f16[8,48,128]{2,1,0:T(8,128)(2,1)S(1)} all-to-all(f16[8,48,128]{2,1,0:T(8,128)(2,1)S(1)} %broadcast_in_dim.11), channel_id=1, replica_groups={{0,16,32,48,64,80,96,112},{8,24,40,56,72,88,104,120},{128,144,160,176,1..., dimensions={0} | all-to-all | bytes 196608 | tf_op jit(solution)/shard_map/all_to_all | solution.py:190
  101.3 0.1 broadcast_in_dim.25
  101.4 14.5 %all_to_all.34 = f16[8,48,1024]{2,1,0:T(8,128)(2,1)S(1)} all-to-all(f16[8,48,1024]{2,1,0:T(8,128)(2,1)S(1)} %broadcast_in_dim.25), channel_id=1, replica_groups={{0,8,128,136,256,264,384,392},{16,24,144,152,272,280,400,408},{32,40,16..., dimensions={0} | all-to-all | bytes 1572864 | tf_op jit(solution)/shard_map/all_to_all | solution.py:190
  115.9 0.0 copy-done.1
  115.9 1.4 %fusion = f32[384,1024]{1,0:T(8,128)} fusion(s32[384,1024]{1,0:T(8,128)S(1)} %copy-done.1, f16[8,48,1024]{2,1,0:T(8,128)(2,1)S(1)} %all_to_all.34, f32[1024]{0:T(1024)S(1)} %bitcast.20), kind=kLoop, calls=%fused_computation.1 | loop fusion | flops 1572864 | bytes 3936256 | tf_op jit(solution)/shard_map/mul | solution.py:272
  (4 shorter events, 0.1 us)
Async XLA Ops:
  0.6 44.2 %copy-start = (s32[16]{0:T(128)S(1)}, s32[16]{0:T(128)}, u32[]{:S(2)}) copy-start(s32[16]{0:T(128)} %level_ref.1) | copy-start | bytes 196
  3.7 53.4 %collective-permute-start = (f32[96,1024]{1,0:T(8,128)S(1)}, f32[96,1024]{1,0:T(8,128)S(1)}, u32[]{:S(2)}, u32[]{:S(2)}) collective-permute-start(f32[96,1024]{1,0:T(8,128)S(1)} %get-tuple-element.16.r1), channel_id=1, source_target_pairs={{0,128},{8,136},{16,144},{24,152},{32,160},{40,168},{48,176},{56,1... | collective-permute-start | bytes 1179656 | tf_op jit(solution)/shard_map/ppermute | solution.py:227
  7.2 49.9 %collective-permute-start.1 = (f32[96,1024]{1,0:T(8,128)S(1)}, f32[96,1024]{1,0:T(8,128)S(1)}, u32[]{:S(2)}, u32[]{:S(2)}) collective-permute-start(f32[96,1024]{1,0:T(8,128)S(1)} %get-tuple-element.17.r2), channel_id=1, source_target_pairs={{0,256},{8,264},{16,272},{24,280},{32,288},{40,296},{48,304},{56,3... | collective-permute-start | bytes 1179656 | tf_op jit(solution)/shard_map/ppermute | solution.py:227
  12.0 45.1 %collective-permute-start.2 = (f32[96,1024]{1,0:T(8,128)S(1)}, f32[96,1024]{1,0:T(8,128)S(1)}, u32[]{:S(2)}, u32[]{:S(2)}) collective-permute-start(f32[96,1024]{1,0:T(8,128)S(1)} %get-tuple-element.18.r3), channel_id=1, source_target_pairs={{0,384},{8,392},{16,400},{24,408},{32,416},{40,424},{48,432},{56,4... | collective-permute-start | bytes 1179656 | tf_op jit(solution)/shard_map/ppermute | solution.py:227
  29.6 27.6 %all-to-all-start.1 = ((f32[16,1,128]{2,1,0:T(1,128)}), f32[16,1,128]{2,1,0:T(1,128)S(1)}, u32[]{:S(2)}, u32[]{:S(2)}) async-start(f32[16,1,128]{2,1,0:T(1,128)} %broadcast_in_dim.10), calls=%async_computation.1 | async-start | bytes 16384 | tf_op jit(solution)/shard_map/all_to_all | solution.py:190
  63.7 19.2 %all-to-all-start.2 = ((f16[16,48,128]{2,1,0:T(8,128)(2,1)}), f16[16,48,128]{2,1,0:T(8,128)(2,1)S(1)}, u32[]{:S(2)}, u32[]{:S(2)}) async-start(f16[16,48,128]{2,1,0:T(8,128)(2,1)} %convert_element_type.22), calls=%async_computation.2 | async-start | bytes 393216 | tf_op jit(solution)/shard_map/all_to_all | solution.py:190
  73.4 42.5 %copy-start.1 = (s32[384,1024]{1,0:T(8,128)S(1)}, s32[384,1024]{1,0:T(8,128)}, u32[]{:S(2)}) copy-start(s32[384,1024]{1,0:T(8,128)} %flip_hbm.1) | copy-start | bytes 4718596

commit v4 on v2

--- a/solution.py
+++ b/solution.py
@@ -126,7 +126,7 @@
             code_ref[pl.ds(row, 16), groups[i][1]] = code.astype(BF16)
         return carry
 
-    lax.fori_loop(0, rows // 16, chunk, 0)
+    lax.fori_loop(0, rows // 16, chunk, 0, unroll=2)
 
 
 def residual_kernel(rot_ref, full_ref, scale_ref, out_ref):
@@ -155,10 +155,15 @@
     replicas, splits = lax.axis_size("dp"), lax.axis_size("fsdp")
     depth = 16
     ys, pairs = range(replicas // depth), range(depth // 2)
+    zs = [(depth // 2 + z) % depth for z in range(depth)]
     near = [[y * depth + 2 * h + l for y in ys for l in range(2)] for h in pairs]
-    far = [[y * depth + 2 * h + l for h in pairs] for y in ys for l in range(2)]
-    line = [[y * depth + z for z in range(depth)] for y in ys]
-    plane = [[(y * depth + z) * splits + f for y in ys for f in range(splits)] for z in range(depth)]
+    far = [[y * depth + z for z in zs[l::2]] for y in ys for l in range(2)]
+    line = [[y * depth + z for z in zs] for y in ys]
+    plane = [
+        [(y * depth + z) * splits + f for y in reversed(ys) for f in range(splits - 2, -1, -1)]
+        + [(y * depth + z) * splits + splits - 1 for y in ys]
+        for z in range(depth)
+    ]
     params = functools.partial(pltpu.CompilerParams, vmem_limit_bytes=VMEM_BYTES)
     hbm, vmem = pl.BlockSpec(memory_space=pltpu.HBM), pl.BlockSpec(memory_space=pltpu.VMEM)
     like = jax.ShapeDtypeStruct
@@ -232,6 +237,7 @@
         name="partial",
     )(codes, matrix)
     partial = grouped(partial.astype(F16), "dp", far)
+    partial, new_residual = lax.optimization_barrier((partial, new_residual))
     mean = jnp.sum(partial.astype(F32), axis=0) * 0.125
     mean = jnp.broadcast_to(mean.astype(F16)[None], partial.shape)
     mean = grouped(mean, "dp", far)

time: 117 us -> 107 us (0.915); the launches traced: 116 us -> 107 us
  waiting for transfers between devices: 20.1 us -> 4.05 us
  starting transfers between devices: 18.2 us -> 27.9 us
    all_to_all x2, waiting for transfers between devices: 20.1 us -> 4.05 us  [grouped(): return lax.all_to_all(pieces, axes, 0, 0, axis_index_groups=groups)]
    all_to_all x2, starting transfers between devices: 18.2 us -> 27.9 us  [grouped(): return lax.all_to_all(pieces, axes, 0, 0, axis_index_groups=groups)]
    mul x1, other arithmetic: 3.1 us -> 1.45 us  [on_device(): mean.reshape(rows, width).astype(F32) * factor * sign_flips.astype(F32)]
where the time goes in v4:
time: 107 us
  blocking collectives  60.2 us (56%)
  starting transfers between devices  27.9 us (26%)
  Pallas kernels  11.1 us (10%)
  waiting for transfers between devices  4.05 us (4%)
  other arithmetic  2.2 us (2%)
    all_to_all x4, blocking collectives, grouped(): return lax.all_to_all(pieces, axes, 0, 0, axis_index_groups=groups)  60.2 us
    all_to_all x2, starting transfers between devices, grouped(): return lax.all_to_all(pieces, axes, 0, 0, axis_index_groups=groups)  27.9 us
    pallas_call x1, Pallas kernels, on_device(): pl.pallas_call(functools.partial(quantize_kernel, replicas), in_specs=[vm...  5.29 us
    all_to_all x2, waiting for transfers between devices, grouped(): return lax.all_to_all(pieces, axes, 0, 0, axis_index_groups=groups)  4.05 us
    pallas_call x1, Pallas kernels, on_device(): pl.pallas_call(rotate_kernel, in_specs=[hbm] * 3, out_specs=[vmem] * 3, o...  3.06 us
  transfers between devices with their start and end apart: 2, of which 2 were waited for; matrix products, arithmetic and copies ran while one was open for 0% of the time, Pallas kernels for 2%

profile of v4, /device:TPU:6, one launch (start us, length us, event | category | flops | bytes accessed | tf_op | source)
XLA Modules:
  0.0 107.0 jit_solution(12205017604398153337)
XLA Ops:
  0.6 0.0 copy-start
  0.6 3.1 %rotate.1 = (f32[384,1024]{1,0:T(8,128)S(1)}, f32[32,128]{1,0:T(8,128)S(1)}, bf16[256,256]{1,0:T(8,128)(2,1)S(1)}) custom-call(f32[384,1024]{1,0:T(8,128)} %bitcast.22, s32[384,1024]{1,0:T(8,128)} %flip_hbm.1, f32[384,1024]{1,0:T(8,128)} %bitcast.23), custom_call_target="tpu_custom_call" | custom-call | tf_op jit(solution)/shard_map/rotate/pallas_call | solution.py:172
  3.7 15.3 %all_to_all.37 = f32[32,1,128]{2,1,0:T(1,128)S(1)} all-to-all(f32[32,1,128]{2,1,0:T(1,128)S(1)} %bitcast.20), channel_id=1, replica_groups={{390,389,388,387,386,385,384,262,261,260,259,258,257,256,134,133,132,13..., dimensions={0} | all-to-all | bytes 32768 | tf_op jit(solution)/shard_map/all_to_all | solution.py:149
  19.0 0.1 reduce_max.9
  19.1 0.6 broadcast_in_dim.10
  19.7 15.4 %all-to-all-start.1 = ((f32[16,1,128]{2,1,0:T(1,128)}), f32[16,1,128]{2,1,0:T(1,128)S(1)}, u32[]{:S(2)}, u32[]{:S(2)}) async-start(f32[16,1,128]{2,1,0:T(1,128)} %broadcast_in_dim.10), calls=%async_computation.1 | async-start | bytes 16384 | tf_op jit(solution)/shard_map/all_to_all | solution.py:149
  35.1 0.0 copy-done
  35.1 0.6 table.1
  35.7 1.8 %all-to-all-done.1 = f32[16,1,128]{2,1,0:T(1,128)S(1)} async-done(((f32[16,1,128]{2,1,0:T(1,128)}), f32[16,1,128]{2,1,0:T(1,128)S(1)}, u32[]{:S(2)}, u32[]{:S(2)}) %all-to-all-start.1) | async-done | bytes 8224 | tf_op jit(solution)/shard_map/all_to_all | solution.py:149
  37.5 5.3 %quantize.1 = (bf16[384,1024]{1,0:T(8,128)(2,1)S(1)}, f32[384,1024]{1,0:T(8,128)S(1)}, f32[8,128]{1,0:T(8,128)S(1)}, f32[1,1024]{1,0:T(1,128)S(1)}) custom-call(f32[16,128]{1,0:T(8,128)S(1)} %bitcast.19, f32[384,1024]{1,0:T(8,128)S(1)} %get-tuple-element.14.rot_ref, f32[16,8,128]{2,1,0:T(8,128)S(1)} %get-tuple-element.15.centre_ref, ...), custom_call_target="tpu_custom_call" | custom-call | tf_op jit(solution)/shard_map/quantize/pallas_call | solution.py:203
  42.8 15.6 %all_to_all.38.codes_ref = bf16[8,48,1024]{2,1,0:T(8,128)(2,1)S(1)} all-to-all(bf16[8,48,1024]{2,1,0:T(8,128)(2,1)S(1)} %bitcast.18), channel_id=1, replica_groups={{0,8,128,136,256,264,384,392},{16,24,144,152,272,280,400,408},{32,40,16..., dimensions={0} | all-to-all | bytes 1572864 | tf_op jit(solution)/shard_map/all_to_all | solution.py:149
  58.4 0.4 partial.1
  58.8 0.7 convert_element_type.22
  59.5 12.5 %all-to-all-start.3 = ((f16[8,48,128]{2,1,0:T(8,128)(2,1)}), f16[8,48,128]{2,1,0:T(8,128)(2,1)S(1)}, u32[]{:S(2)}, u32[]{:S(2)}) async-start(f16[8,48,128]{2,1,0:T(8,128)(2,1)} %convert_element_type.22), calls=%async_computation.3 | async-start | bytes 196608 | tf_op jit(solution)/shard_map/all_to_all | solution.py:149
  72.0 1.8 %residual.1 = f32[384,1024]{1,0:T(8,128)} custom-call(f32[384,1024]{1,0:T(8,128)S(1)} %get-tuple-element.14.rot_ref, f32[384,1024]{1,0:T(8,128)S(1)} %get-tuple-element.19.full_ref, f32[8,128]{1,0:T(8,128)S(1)} %get-tuple-element.20.scale_ref), custom_call_target="tpu_custom_call" | custom-call | flops 786432 | bytes 4718592 | tf_op jit(solution)/shard_map/residual/pallas_call | solution.py:219
  73.8 0.0 copy-start.1
  73.8 2.3 %all-to-all-done.3 = f16[8,48,128]{2,1,0:T(8,128)(2,1)S(1)} async-done(((f16[8,48,128]{2,1,0:T(8,128)(2,1)}), f16[8,48,128]{2,1,0:T(8,128)(2,1)S(1)}, u32[]{:S(2)}, u32[]{:S(2)}) %all-to-all-start.3) | async-done | bytes 98336 | tf_op jit(solution)/shard_map/all_to_all | solution.py:149
  76.1 16.2 %all_to_all.39 = f16[8,48,128]{2,1,0:T(8,128)(2,1)S(1)} all-to-all(f16[8,48,128]{2,1,0:T(8,128)(2,1)S(1)} %broadcast_in_dim.11), channel_id=1, replica_groups={{64,80,96,112,0,16,32,48},{72,88,104,120,8,24,40,56},{192,208,224,240,1..., dimensions={0} | all-to-all | bytes 196608 | tf_op jit(solution)/shard_map/all_to_all | solution.py:149
  92.3 0.1 broadcast_in_dim.25
  92.4 13.2 %all_to_all.40 = f16[8,48,1024]{2,1,0:T(8,128)(2,1)S(1)} all-to-all(f16[8,48,1024]{2,1,0:T(8,128)(2,1)S(1)} %broadcast_in_dim.25), channel_id=1, replica_groups={{0,8,128,136,256,264,384,392},{16,24,144,152,272,280,400,408},{32,40,16..., dimensions={0} | all-to-all | bytes 1572864 | tf_op jit(solution)/shard_map/all_to_all | solution.py:149
  105.6 0.0 copy-done.1
  105.6 1.4 %fusion = f32[384,1024]{1,0:T(8,128)} fusion(s32[384,1024]{1,0:T(8,128)S(1)} %copy-done.1, f16[8,48,1024]{2,1,0:T(8,128)(2,1)S(1)} %all_to_all.40, f32[1024]{0:T(1024)S(1)} %bitcast.21), kind=kLoop, calls=%fused_computation.1 | loop fusion | flops 1572864 | bytes 3936256 | tf_op jit(solution)/shard_map/mul | solution.py:246
  (4 shorter events, 0.1 us)
Async XLA Ops:
  0.6 34.5 %copy-start = (s32[16]{0:T(128)S(1)}, s32[16]{0:T(128)}, u32[]{:S(2)}) copy-start(s32[16]{0:T(128)} %level_ref.1) | copy-start | bytes 196
  19.7 17.8 %all-to-all-start.1 = ((f32[16,1,128]{2,1,0:T(1,128)}), f32[16,1,128]{2,1,0:T(1,128)S(1)}, u32[]{:S(2)}, u32[]{:S(2)}) async-start(f32[16,1,128]{2,1,0:T(1,128)} %broadcast_in_dim.10), calls=%async_computation.1 | async-start | bytes 16384 | tf_op jit(solution)/shard_map/all_to_all | solution.py:149
  59.5 16.6 %all-to-all-start.3 = ((f16[8,48,128]{2,1,0:T(8,128)(2,1)}), f16[8,48,128]{2,1,0:T(8,128)(2,1)S(1)}, u32[]{:S(2)}, u32[]{:S(2)}) async-start(f16[8,48,128]{2,1,0:T(8,128)(2,1)} %convert_element_type.22), calls=%async_computation.3 | async-start | bytes 196608 | tf_op jit(solution)/shard_map/all_to_all | solution.py:149
  73.8 31.8 %copy-start.1 = (s32[384,1024]{1,0:T(8,128)S(1)}, s32[384,1024]{1,0:T(8,128)}, u32[]{:S(2)}) copy-start(s32[384,1024]{1,0:T(8,128)} %flip_hbm.1) | copy-start | bytes 4718596

commit v5 on v4

--- a/solution.py
+++ b/solution.py
@@ -27,7 +27,7 @@
     return (1 - 2 * (common & 1)).astype(F32).astype(BF16)
 
 
-def turn(values, matrix, scale):
+def butterflies(values):
     count = values.shape[1] // FOLD
     parts = [values[:, k * FOLD : (k + 1) * FOLD] for k in range(count)]
     step = 1
@@ -39,16 +39,16 @@
                 nxt[k + step] = parts[k] - parts[k + step]
         parts = nxt
         step *= 2
-    turned = []
-    for part in parts:
-        part = part * scale
-        high = part.astype(BF16)
-        rest = part - high.astype(F32)
-        middle = rest.astype(BF16)
-        low = (rest - middle.astype(F32)).astype(BF16)
-        dot = functools.partial(jnp.dot, preferred_element_type=F32)
-        turned.append(dot(high, matrix) + (dot(middle, matrix) + dot(low, matrix)))
-    return turned
+    return parts
+
+
+def turn(part, matrix):
+    high = part.astype(BF16)
+    rest = part - high.astype(F32)
+    middle = rest.astype(BF16)
+    low = (rest - middle.astype(F32)).astype(BF16)
+    dot = functools.partial(jnp.dot, preferred_element_type=F32)
+    return dot(high, matrix) + (dot(middle, matrix) + dot(low, matrix))
 
 
 def rotate_kernel(
@@ -74,9 +74,9 @@
             copy.wait()
         at = slice(c * deep, (c + 1) * deep)
         signed = grad[at, :] * flip[at, :].astype(F32)
-        for k, part in enumerate(turn(signed, matrix_ref[...], 1.0 / math.sqrt(width))):
+        for k, part in enumerate(butterflies(signed * (1.0 / math.sqrt(width)))):
             cols = slice(k * FOLD, (k + 1) * FOLD)
-            rotated = part + resid[at, cols]
+            rotated = turn(part, matrix_ref[...]) + resid[at, cols]
             rot_ref[at, cols] = rotated
             size = jnp.abs(rotated)
             for lane in range(0, FOLD, LANES):
@@ -85,19 +85,17 @@
     peak_ref[...] = jnp.broadcast_to(jnp.max(top, axis=0, keepdims=True), peak_ref.shape)
 
 
-def table_kernel(level_ref, centre_ref, lift_ref):
-    count = level_ref.shape[0]
-    bottom = level_ref[0].astype(F32)
-    upper = level_ref[count - 1].astype(F32)
-    middle = (bottom + upper) * 0.5
+def quantize_kernel(
+    replicas, peaks_ref, rot_ref, level_ref, code_ref, full_ref, scale_ref, factor_ref, centre_ref, lift_ref
+):
+    count = level_ref.shape[1]
+    levels = level_ref[...].astype(F32)
+    bottom, upper = levels[:, 0:1], levels[:, count - 1 : count]
+    centred = levels - (bottom + upper) * 0.5
+    lift = centred * centred * (-LOG2E / 72.0)
     for k in range(count):
-        centred = jnp.full((8, LANES), level_ref[k].astype(F32) - middle, F32)
-        centre_ref[k] = centred
-        lift_ref[k] = centred * centred * (-LOG2E / 72.0)
-
-
-def quantize_kernel(replicas, peaks_ref, rot_ref, centre_ref, lift_ref, code_ref, full_ref, scale_ref, factor_ref):
-    count = centre_ref.shape[0]
+        centre_ref[k] = jnp.broadcast_to(centred[:, k : k + 1], (8, LANES))
+        lift_ref[k] = jnp.broadcast_to(lift[:, k : k + 1], (8, LANES))
     rows, width = rot_ref.shape
     top = jnp.max(peaks_ref[...], axis=0, keepdims=True)
     peak = jnp.max(top, axis=1, keepdims=True) + 1e-06
@@ -139,8 +137,9 @@
     total = codes_ref[0].astype(F32)
     for k in range(1, codes_ref.shape[0]):
         total = total + codes_ref[k].astype(F32)
-    turned = turn(total, matrix_ref[...], 1.0 / math.sqrt(width))
-    for k, part in enumerate(turned):
+    parts = butterflies(total * (1.0 / math.sqrt(width)))
+    turned = turn(jnp.concatenate(parts, axis=0), matrix_ref[...])
+    for k, part in enumerate(jnp.split(turned, len(parts), axis=0)):
         for at in range(0, FOLD, LANES):
             out_ref[(k * FOLD + at) // LANES] = part[:, at : at + LANES]
 
@@ -155,10 +154,10 @@
     replicas, splits = lax.axis_size("dp"), lax.axis_size("fsdp")
     depth = 16
     ys, pairs = range(replicas // depth), range(depth // 2)
-    zs = [(depth // 2 + z) % depth for z in range(depth)]
-    near = [[y * depth + 2 * h + l for y in ys for l in range(2)] for h in pairs]
-    far = [[y * depth + z for z in zs[l::2]] for y in ys for l in range(2)]
-    line = [[y * depth + z for z in zs] for y in ys]
+    ring = sorted(range(depth), key=lambda z: (z != depth // 2, -min((z - depth // 2) % depth, (depth // 2 - z) % depth)))
+    near = [[y * depth + 2 * h + l for y in reversed(ys) for l in range(2)] for h in pairs]
+    far = [[y * depth + z + l for z in ring if z % 2 == 0] for y in ys for l in range(2)]
+    line = [[y * depth + z for z in ring] for y in ys]
     plane = [
         [(y * depth + z) * splits + f for y in reversed(ys) for f in range(splits - 2, -1, -1)]
         + [(y * depth + z) * splits + splits - 1 for y in ys]
@@ -187,22 +186,13 @@
         compiler_params=pltpu.CompilerParams(vmem_limit_bytes=ROTATE_BYTES),
         name="rotate",
     )(gradient[0], sign_flips, residual[0])
-    centred, lift = pl.pallas_call(
-        table_kernel,
-        in_specs=[pl.BlockSpec(memory_space=pltpu.SMEM)],
-        out_specs=[vmem] * 2,
-        out_shape=[like((levels, 8, LANES), F32)] * 2,
-        compiler_params=params(),
-        name="table",
-    )(level_table)
-
     peaks = grouped(peaks, ("dp", "fsdp"), plane)
     peaks = jnp.broadcast_to(jnp.max(peaks, axis=0, keepdims=True), (depth, LANES))
     peaks = grouped(peaks, "dp", line)
 
     codes, full, scale, factor = pl.pallas_call(
         functools.partial(quantize_kernel, replicas),
-        in_specs=[vmem] * 4,
+        in_specs=[vmem] * 3,
         out_specs=[vmem] * 4,
         out_shape=[
             like((rows, width), BF16),
@@ -210,9 +200,10 @@
             like((8, LANES), F32),
             like((1, width), F32),
         ],
+        scratch_shapes=[pltpu.VMEM((levels, 8, LANES), F32)] * 2,
         compiler_params=params(),
         name="quantize",
-    )(peaks, rotated, centred, lift)
+    )(peaks, rotated, level_table.reshape(1, levels))
 
     block = 96
     tile = pl.BlockSpec((block, width), lambda i: (i, 0))

time: 107 us -> 105 us (0.981)
  blocking collectives: 60.2 us -> 76 us
  starting transfers between devices: 27.9 us -> 12.9 us
  waiting for transfers between devices: 4.05 us -> 2.38 us
    all_to_all x4 -> x5, blocking collectives: 60.2 us -> 76 us  [grouped(): return lax.all_to_all(pieces, axes, 0, 0, axis_index_groups=groups)]
    all_to_all x2 -> x1, starting transfers between devices: 27.9 us -> 12.9 us  [grouped(): return lax.all_to_all(pieces, axes, 0, 0, axis_index_groups=groups)]
    all_to_all x2 -> x1, waiting for transfers between devices: 4.05 us -> 2.38 us  [grouped(): return lax.all_to_all(pieces, axes, 0, 0, axis_index_groups=groups)]
  transfers between devices with their start and end apart: 2 -> 1, of which waited for: 2 -> 1; matrix products, arithmetic and copies ran while one was open for 0% -> 0% of each run, Pallas kernels for 2% -> 2%
where the time goes in v5:
time: 105 us
  blocking collectives  76 us (72%)
  starting transfers between devices  12.9 us (12%)
  Pallas kernels  10.7 us (10%)
  waiting for transfers between devices  2.38 us (2%)
  other arithmetic  2.18 us (2%)
    all_to_all x5, blocking collectives, grouped(): return lax.all_to_all(pieces, axes, 0, 0, axis_index_groups=groups)  76 us
    all_to_all x1, starting transfers between devices, grouped(): return lax.all_to_all(pieces, axes, 0, 0, axis_index_groups=groups)  12.9 us
    pallas_call x1, Pallas kernels, on_device(): pl.pallas_call(functools.partial(quantize_kernel, replicas), in_specs=[vm...  5.44 us
    pallas_call x1, Pallas kernels, on_device(): pl.pallas_call(rotate_kernel, in_specs=[hbm] * 3, out_specs=[vmem] * 3, o...  3.1 us
    all_to_all x1, waiting for transfers between devices, grouped(): return lax.all_to_all(pieces, axes, 0, 0, axis_index_groups=groups)  2.38 us
  transfers between devices with their start and end apart: 1, of which 1 were waited for; matrix products, arithmetic and copies ran while one was open for 0% of the time, Pallas kernels for 2%

profile of v5, /device:TPU:6, one launch (start us, length us, event | category | flops | bytes accessed | tf_op | source)
XLA Modules:
  0.0 104.9 jit_solution(9006933692095174624)
XLA Ops:
  0.6 0.0 copy-start
  0.6 3.1 %rotate.1 = (f32[384,1024]{1,0:T(8,128)S(1)}, f32[32,128]{1,0:T(8,128)S(1)}, bf16[256,256]{1,0:T(8,128)(2,1)S(1)}) custom-call(f32[384,1024]{1,0:T(8,128)} %bitcast.24, s32[384,1024]{1,0:T(8,128)} %flip_hbm.1, f32[384,1024]{1,0:T(8,128)} %bitcast.25), custom_call_target="tpu_custom_call" | custom-call | tf_op jit(solution)/shard_map/rotate/pallas_call | solution.py:171
  3.7 15.3 %all_to_all.37 = f32[32,1,128]{2,1,0:T(1,128)S(1)} all-to-all(f32[32,1,128]{2,1,0:T(1,128)S(1)} %bitcast.21), channel_id=1, replica_groups={{390,389,388,387,386,385,384,262,261,260,259,258,257,256,134,133,132,13..., dimensions={0} | all-to-all | bytes 32768 | tf_op jit(solution)/shard_map/all_to_all | solution.py:148
  19.1 0.1 reduce_max.9
  19.1 17.6 %all_to_all.38 = f32[16,1,128]{2,1,0:T(1,128)S(1)} all-to-all(f32[16,1,128]{2,1,0:T(1,128)S(1)} %broadcast_in_dim.10), channel_id=1, replica_groups={{64,0,8,120,16,112,24,104,32,96,40,88,48,80,56,72},{192,128,136,248,144..., dimensions={0} | all-to-all | bytes 16384 | tf_op jit(solution)/shard_map/all_to_all | solution.py:148
  36.8 0.0 copy-done
  36.8 5.4 %quantize.1 = (bf16[384,1024]{1,0:T(8,128)(2,1)S(1)}, f32[384,1024]{1,0:T(8,128)S(1)}, f32[8,128]{1,0:T(8,128)S(1)}, f32[1,1024]{1,0:T(1,128)S(1)}) custom-call(f32[16,128]{1,0:T(8,128)S(1)} %bitcast.20, f32[384,1024]{1,0:T(8,128)S(1)} %get-tuple-element.12.rot_ref, s32[1,16]{1,0:T(1,128)S(1)} %bitcast.23), custom_call_target="tpu_custom_call" | custom-call | tf_op jit(solution)/shard_map/quantize/pallas_call | solution.py:193
  42.2 14.3 %all_to_all.39.codes_ref = bf16[8,48,1024]{2,1,0:T(8,128)(2,1)S(1)} all-to-all(bf16[8,48,1024]{2,1,0:T(8,128)(2,1)S(1)} %bitcast.19), channel_id=1, replica_groups={{384,392,256,264,128,136,0,8},{400,408,272,280,144,152,16,24},{416,424,..., dimensions={0} | all-to-all | bytes 1572864 | tf_op jit(solution)/shard_map/all_to_all | solution.py:148
  56.5 0.3 partial.1
  56.9 0.7 convert_element_type.22
  57.5 12.9 %all-to-all-start.3 = ((f16[8,48,128]{2,1,0:T(8,128)(2,1)}), f16[8,48,128]{2,1,0:T(8,128)(2,1)S(1)}, u32[]{:S(2)}, u32[]{:S(2)}) async-start(f16[8,48,128]{2,1,0:T(8,128)(2,1)} %convert_element_type.22), calls=%async_computation.3 | async-start | bytes 196608 | tf_op jit(solution)/shard_map/all_to_all | solution.py:148
  70.4 1.8 %residual.1 = f32[384,1024]{1,0:T(8,128)} custom-call(f32[384,1024]{1,0:T(8,128)S(1)} %get-tuple-element.12.rot_ref, f32[384,1024]{1,0:T(8,128)S(1)} %get-tuple-element.15.full_ref, f32[8,128]{1,0:T(8,128)S(1)} %get-tuple-element.16.scale_ref), custom_call_target="tpu_custom_call" | custom-call | flops 786432 | bytes 4718592 | tf_op jit(solution)/shard_map/residual/pallas_call | solution.py:210
  72.2 0.0 copy-start.1
  72.2 2.4 %all-to-all-done.3 = f16[8,48,128]{2,1,0:T(8,128)(2,1)S(1)} async-done(((f16[8,48,128]{2,1,0:T(8,128)(2,1)}), f16[8,48,128]{2,1,0:T(8,128)(2,1)S(1)}, u32[]{:S(2)}, u32[]{:S(2)}) %all-to-all-start.3) | async-done | bytes 98336 | tf_op jit(solution)/shard_map/all_to_all | solution.py:148
  74.6 16.0 %all_to_all.40 = f16[8,48,128]{2,1,0:T(8,128)(2,1)S(1)} all-to-all(f16[8,48,128]{2,1,0:T(8,128)(2,1)S(1)} %broadcast_in_dim.11), channel_id=1, replica_groups={{64,0,16,112,32,96,48,80},{72,8,24,120,40,104,56,88},{192,128,144,240,1..., dimensions={0} | all-to-all | bytes 196608 | tf_op jit(solution)/shard_map/all_to_all | solution.py:148
  90.6 0.1 broadcast_in_dim.25
  90.7 12.8 %all_to_all.41 = f16[8,48,1024]{2,1,0:T(8,128)(2,1)S(1)} all-to-all(f16[8,48,1024]{2,1,0:T(8,128)(2,1)S(1)} %broadcast_in_dim.25), channel_id=1, replica_groups={{384,392,256,264,128,136,0,8},{400,408,272,280,144,152,16,24},{416,424,..., dimensions={0} | all-to-all | bytes 1572864 | tf_op jit(solution)/shard_map/all_to_all | solution.py:148
  103.5 0.0 copy-done.1
  103.5 1.4 %fusion = f32[384,1024]{1,0:T(8,128)} fusion(s32[384,1024]{1,0:T(8,128)S(1)} %copy-done.1, f16[8,48,1024]{2,1,0:T(8,128)(2,1)S(1)} %all_to_all.41, f32[1024]{0:T(1024)S(1)} %bitcast.22), kind=kLoop, calls=%fused_computation.1 | loop fusion | flops 1572864 | bytes 3936256 | tf_op jit(solution)/shard_map/mul | solution.py:237
  (5 shorter events, 0.1 us)
Async XLA Ops:
  0.6 36.1 %copy-start = (s32[16]{0:T(128)S(1)}, s32[16]{0:T(128)}, u32[]{:S(2)}) copy-start(s32[16]{0:T(128)} %param.7) | copy-start | bytes 196
  57.5 17.1 %all-to-all-start.3 = ((f16[8,48,128]{2,1,0:T(8,128)(2,1)}), f16[8,48,128]{2,1,0:T(8,128)(2,1)S(1)}, u32[]{:S(2)}, u32[]{:S(2)}) async-start(f16[8,48,128]{2,1,0:T(8,128)(2,1)} %convert_element_type.22), calls=%async_computation.3 | async-start | bytes 196608 | tf_op jit(solution)/shard_map/all_to_all | solution.py:148
  72.2 31.3 %copy-start.1 = (s32[384,1024]{1,0:T(8,128)S(1)}, s32[384,1024]{1,0:T(8,128)}, u32[]{:S(2)}) copy-start(s32[384,1024]{1,0:T(8,128)} %flip_hbm.1) | copy-start | bytes 4718596

commit v6 on v5

--- a/solution.py
+++ b/solution.py
@@ -132,16 +132,16 @@
     out_ref[...] = rot_ref[...] - full_ref[...] * scale
 
 
-def partial_kernel(codes_ref, matrix_ref, out_ref):
+def partial_kernel(chunk_of, codes_ref, matrix_ref, out_ref):
     width = codes_ref.shape[2]
     total = codes_ref[0].astype(F32)
     for k in range(1, codes_ref.shape[0]):
         total = total + codes_ref[k].astype(F32)
     parts = butterflies(total * (1.0 / math.sqrt(width)))
     turned = turn(jnp.concatenate(parts, axis=0), matrix_ref[...])
-    for k, part in enumerate(jnp.split(turned, len(parts), axis=0)):
-        for at in range(0, FOLD, LANES):
-            out_ref[(k * FOLD + at) // LANES] = part[:, at : at + LANES]
+    chunks = jnp.split(turned, len(parts), axis=0)
+    for i, chunk in enumerate(chunk_of):
+        out_ref[i] = chunks[chunk]
 
 
 def grouped(pieces, axes, groups):
@@ -157,6 +157,9 @@
     ring = sorted(range(depth), key=lambda z: (z != depth // 2, -min((z - depth // 2) % depth, (depth // 2 - z) % depth)))
     near = [[y * depth + 2 * h + l for y in reversed(ys) for l in range(2)] for h in pairs]
     far = [[y * depth + z + l for z in ring if z % 2 == 0] for y in ys for l in range(2)]
+    halves = ((8, 4, 10, 6), (14, 2, 12, 0))
+    half = [[y * depth + z + l for z in members] for members in halves for y in ys for l in range(2)]
+    chunk_of = [members.index(z) for z in ring if z % 2 == 0 for members in halves if z in members]
     line = [[y * depth + z for z in ring] for y in ys]
     plane = [
         [(y * depth + z) * splits + f for y in reversed(ys) for f in range(splits - 2, -1, -1)]
@@ -218,20 +221,20 @@
         name="residual",
     )(rotated, full, scale)
 
-    first, second = len(near[0]), len(far[0])
+    first, second, third = len(near[0]), len(far[0]), len(half[0])
     share = rows // first
     codes = grouped(codes.reshape(first, share, width), "dp", near)
     partial = pl.pallas_call(
-        partial_kernel,
-        out_shape=like((second, share, width // second), F32),
+        functools.partial(partial_kernel, chunk_of),
+        out_shape=like((second, share, width // third), F32),
         compiler_params=params(),
         name="partial",
     )(codes, matrix)
     partial = grouped(partial.astype(F16), "dp", far)
     partial, new_residual = lax.optimization_barrier((partial, new_residual))
     mean = jnp.sum(partial.astype(F32), axis=0) * 0.125
-    mean = jnp.broadcast_to(mean.astype(F16)[None], partial.shape)
-    mean = grouped(mean, "dp", far)
+    mean = jnp.broadcast_to(mean.astype(F16)[None], (third,) + mean.shape)
+    mean = grouped(mean, "dp", half)
     mean = mean.transpose(1, 0, 2).reshape(share, width)
     mean = grouped(jnp.broadcast_to(mean[None], (first, share, width)), "dp", near)
     mean = mean.reshape(rows, width).astype(F32) * factor * sign_flips.astype(F32)

time: 105 us -> 105 us (level)
  blocking collectives: 76 us -> 72.1 us
  waiting for transfers between devices: 2.38 us -> 5.52 us
    all_to_all x5, blocking collectives: 76 us -> 72.1 us  [grouped(): return lax.all_to_all(pieces, axes, 0, 0, axis_index_groups=groups)]
    all_to_all x1, waiting for transfers between devices: 2.38 us -> 5.52 us  [grouped(): return lax.all_to_all(pieces, axes, 0, 0, axis_index_groups=groups)]
where the time goes in v6:
time: 105 us; the launch traced here: 104 us
  blocking collectives  72.1 us (69%)
  starting transfers between devices  12.9 us (12%)
  Pallas kernels  10.7 us (10%)
  waiting for transfers between devices  5.52 us (5%)
  other arithmetic  2.34 us (2%)
    all_to_all x5, blocking collectives, grouped(): return lax.all_to_all(pieces, axes, 0, 0, axis_index_groups=groups)  72.1 us
    all_to_all x1, starting transfers between devices, grouped(): return lax.all_to_all(pieces, axes, 0, 0, axis_index_groups=groups)  12.9 us
    all_to_all x1, waiting for transfers between devices, grouped(): return lax.all_to_all(pieces, axes, 0, 0, axis_index_groups=groups)  5.52 us
    pallas_call x1, Pallas kernels, on_device(): pl.pallas_call(functools.partial(quantize_kernel, replicas), in_specs=[vm...  5.46 us
    pallas_call x1, Pallas kernels, on_device(): pl.pallas_call(rotate_kernel, in_specs=[hbm] * 3, out_specs=[vmem] * 3, o...  3.11 us
  transfers between devices with their start and end apart: 1, of which 1 were waited for; matrix products, arithmetic and copies ran while one was open for 0% of the time, Pallas kernels for 2%

profile of v6, /device:TPU:6, one launch (start us, length us, event | category | flops | bytes accessed | tf_op | source)
XLA Modules:
  0.0 104.4 jit_solution(2889851625605455782)
XLA Ops:
  0.6 0.0 copy-start
  0.6 3.1 %rotate.1 = (f32[384,1024]{1,0:T(8,128)S(1)}, f32[32,128]{1,0:T(8,128)S(1)}, bf16[256,256]{1,0:T(8,128)(2,1)S(1)}) custom-call(f32[384,1024]{1,0:T(8,128)} %bitcast.21, s32[384,1024]{1,0:T(8,128)} %flip_hbm.1, f32[384,1024]{1,0:T(8,128)} %bitcast.22), custom_call_target="tpu_custom_call" | custom-call | tf_op jit(solution)/shard_map/rotate/pallas_call | solution.py:174
  3.8 15.3 %all_to_all.37 = f32[32,1,128]{2,1,0:T(1,128)S(1)} all-to-all(f32[32,1,128]{2,1,0:T(1,128)S(1)} %bitcast.18), channel_id=1, replica_groups={{390,389,388,387,386,385,384,262,261,260,259,258,257,256,134,133,132,13..., dimensions={0} | all-to-all | bytes 32768 | tf_op jit(solution)/shard_map/all_to_all | solution.py:148
  19.1 0.1 reduce_max.9
  19.1 17.6 %all_to_all.38 = f32[16,1,128]{2,1,0:T(1,128)S(1)} all-to-all(f32[16,1,128]{2,1,0:T(1,128)S(1)} %broadcast_in_dim.10), channel_id=1, replica_groups={{64,0,8,120,16,112,24,104,32,96,40,88,48,80,56,72},{192,128,136,248,144..., dimensions={0} | all-to-all | bytes 16384 | tf_op jit(solution)/shard_map/all_to_all | solution.py:148
  36.8 0.0 copy-done
  36.8 5.5 %quantize.1 = (bf16[384,1024]{1,0:T(8,128)(2,1)S(1)}, f32[384,1024]{1,0:T(8,128)S(1)}, f32[8,128]{1,0:T(8,128)S(1)}, f32[1,1024]{1,0:T(1,128)S(1)}) custom-call(f32[16,128]{1,0:T(8,128)S(1)} %bitcast.17, f32[384,1024]{1,0:T(8,128)S(1)} %get-tuple-element.12.rot_ref, s32[1,16]{1,0:T(1,128)S(1)} %bitcast.20), custom_call_target="tpu_custom_call" | custom-call | tf_op jit(solution)/shard_map/quantize/pallas_call | solution.py:196
  42.2 14.3 %all_to_all.39.codes_ref = bf16[8,48,1024]{2,1,0:T(8,128)(2,1)S(1)} all-to-all(bf16[8,48,1024]{2,1,0:T(8,128)(2,1)S(1)} %bitcast.16), channel_id=1, replica_groups={{384,392,256,264,128,136,0,8},{400,408,272,280,144,152,16,24},{416,424,..., dimensions={0} | all-to-all | bytes 1572864 | tf_op jit(solution)/shard_map/all_to_all | solution.py:148
  56.5 0.3 partial.1
  56.9 0.7 convert_element_type.22
  57.6 12.9 %all-to-all-start.3 = ((f16[8,48,256]{2,1,0:T(8,128)(2,1)}), f16[8,48,256]{2,1,0:T(8,128)(2,1)S(1)}, u32[]{:S(2)}, u32[]{:S(2)}) async-start(f16[8,48,256]{2,1,0:T(8,128)(2,1)} %convert_element_type.22), calls=%async_computation.3 | async-start | bytes 393216 | tf_op jit(solution)/shard_map/all_to_all | solution.py:148
  70.5 1.8 %residual.1 = f32[384,1024]{1,0:T(8,128)} custom-call(f32[384,1024]{1,0:T(8,128)S(1)} %get-tuple-element.12.rot_ref, f32[384,1024]{1,0:T(8,128)S(1)} %get-tuple-element.15.full_ref, f32[8,128]{1,0:T(8,128)S(1)} %get-tuple-element.16.scale_ref), custom_call_target="tpu_custom_call" | custom-call | flops 786432 | bytes 4718592 | tf_op jit(solution)/shard_map/residual/pallas_call | solution.py:213
  72.3 5.5 %all-to-all-done.3 = f16[8,48,256]{2,1,0:T(8,128)(2,1)S(1)} async-done(((f16[8,48,256]{2,1,0:T(8,128)(2,1)}), f16[8,48,256]{2,1,0:T(8,128)(2,1)S(1)}, u32[]{:S(2)}, u32[]{:S(2)}) %all-to-all-start.3) | async-done | bytes 196640 | tf_op jit(solution)/shard_map/all_to_all | solution.py:148
  77.9 0.0 copy-start.1
  77.9 12.8 %all_to_all.40 = f16[4,48,256]{2,1,0:T(8,128)(2,1)S(1)} all-to-all(f16[4,48,256]{2,1,0:T(8,128)(2,1)S(1)} %broadcast_in_dim.11), channel_id=1, replica_groups={{64,32,80,48},{72,40,88,56},{192,160,208,176},{200,168,216,184},{320,28..., dimensions={0} | all-to-all | bytes 196608 | tf_op jit(solution)/shard_map/all_to_all | solution.py:148
  90.7 0.1 broadcast_in_dim.25
  90.8 12.1 %all_to_all.41 = f16[8,48,1024]{2,1,0:T(8,128)(2,1)S(1)} all-to-all(f16[8,48,1024]{2,1,0:T(8,128)(2,1)S(1)} %broadcast_in_dim.25), channel_id=1, replica_groups={{384,392,256,264,128,136,0,8},{400,408,272,280,144,152,16,24},{416,424,..., dimensions={0} | all-to-all | bytes 1572864 | tf_op jit(solution)/shard_map/all_to_all | solution.py:148
  102.9 0.0 copy-done.1
  102.9 1.5 %fusion = f32[384,1024]{1,0:T(8,128)} fusion(s32[384,1024]{1,0:T(8,128)S(1)} %copy-done.1, f16[8,48,1024]{2,1,0:T(8,128)(2,1)S(1)} %all_to_all.41, f32[1024]{0:T(1024)S(1)} %bitcast.19), kind=kLoop, calls=%fused_computation.1 | loop fusion | flops 1572864 | bytes 3936256 | tf_op jit(solution)/shard_map/mul | solution.py:240
  (5 shorter events, 0.1 us)
Async XLA Ops:
  0.6 36.2 %copy-start = (s32[16]{0:T(128)S(1)}, s32[16]{0:T(128)}, u32[]{:S(2)}) copy-start(s32[16]{0:T(128)} %param.7) | copy-start | bytes 196
  57.6 20.2 %all-to-all-start.3 = ((f16[8,48,256]{2,1,0:T(8,128)(2,1)}), f16[8,48,256]{2,1,0:T(8,128)(2,1)S(1)}, u32[]{:S(2)}, u32[]{:S(2)}) async-start(f16[8,48,256]{2,1,0:T(8,128)(2,1)} %convert_element_type.22), calls=%async_computation.3 | async-start | bytes 393216 | tf_op jit(solution)/shard_map/all_to_all | solution.py:148
  77.9 25.0 %copy-start.1 = (s32[384,1024]{1,0:T(8,128)S(1)}, s32[384,1024]{1,0:T(8,128)}, u32[]{:S(2)}) copy-start(s32[384,1024]{1,0:T(8,128)} %flip_hbm.1) | copy-start | bytes 4718596

commit v7 on v6

--- a/solution.py
+++ b/solution.py
@@ -154,18 +154,18 @@
     replicas, splits = lax.axis_size("dp"), lax.axis_size("fsdp")
     depth = 16
     ys, pairs = range(replicas // depth), range(depth // 2)
-    ring = sorted(range(depth), key=lambda z: (z != depth // 2, -min((z - depth // 2) % depth, (depth // 2 - z) % depth)))
-    near = [[y * depth + 2 * h + l for y in reversed(ys) for l in range(2)] for h in pairs]
-    far = [[y * depth + z + l for z in ring if z % 2 == 0] for y in ys for l in range(2)]
-    halves = ((8, 4, 10, 6), (14, 2, 12, 0))
+    def by_distance(lead):
+        return sorted(range(depth), key=lambda z: (z != lead, -min((z - lead) % depth, (lead - z) % depth)))
+
+    far_ring = by_distance(8)
+    near = [[y * depth + 2 * h + l for y in (2, 1, 3, 0) for l in range(2)] for h in pairs]
+    far = [[y * depth + z + l for z in far_ring if z % 2 == 0] for y in ys for l in range(2)]
+    halves = ((8, 4, 10, 6), (14, 0, 2, 12))
     half = [[y * depth + z + l for z in members] for members in halves for y in ys for l in range(2)]
-    chunk_of = [members.index(z) for z in ring if z % 2 == 0 for members in halves if z in members]
-    line = [[y * depth + z for z in ring] for y in ys]
-    plane = [
-        [(y * depth + z) * splits + f for y in reversed(ys) for f in range(splits - 2, -1, -1)]
-        + [(y * depth + z) * splits + splits - 1 for y in ys]
-        for z in range(depth)
-    ]
+    chunk_of = [members.index(z) for z in far_ring if z % 2 == 0 for members in halves if z in members]
+    line = [[y * depth + z for z in by_distance(10)] for y in ys]
+    spots = sorted(((y, f) for y in ys for f in range(splits)), key=lambda spot: spot != (2, 4))
+    plane = [[(y * depth + z) * splits + f for y, f in spots] for z in range(depth)]
     params = functools.partial(pltpu.CompilerParams, vmem_limit_bytes=VMEM_BYTES)
     hbm, vmem = pl.BlockSpec(memory_space=pltpu.HBM), pl.BlockSpec(memory_space=pltpu.VMEM)
     like = jax.ShapeDtypeStruct

time: 105 us -> 103 us (0.981)
  no operation moved by 1% of the time
where the time goes in v7:
time: 103 us; the launch traced here: 102 us
  blocking collectives  71.2 us (69%)
  starting transfers between devices  12 us (12%)
  Pallas kernels  10.7 us (10%)
  waiting for transfers between devices  5.3 us (5%)
  other arithmetic  2.34 us (2%)
    all_to_all x5, blocking collectives, grouped(): return lax.all_to_all(pieces, axes, 0, 0, axis_index_groups=groups)  71.2 us
    all_to_all x1, starting transfers between devices, grouped(): return lax.all_to_all(pieces, axes, 0, 0, axis_index_groups=groups)  12 us
    pallas_call x1, Pallas kernels, on_device(): pl.pallas_call(functools.partial(quantize_kernel, replicas), in_specs=[vm...  5.46 us
    all_to_all x1, waiting for transfers between devices, grouped(): return lax.all_to_all(pieces, axes, 0, 0, axis_index_groups=groups)  5.3 us
    pallas_call x1, Pallas kernels, on_device(): pl.pallas_call(rotate_kernel, in_specs=[hbm] * 3, out_specs=[vmem] * 3, o...  3.11 us
  transfers between devices with their start and end apart: 1, of which 1 were waited for; matrix products, arithmetic and copies ran while one was open for 0% of the time, Pallas kernels for 2%

profile of v7, /device:TPU:6, one launch (start us, length us, event | category | flops | bytes accessed | tf_op | source)
XLA Modules:
  0.0 102.4 jit_solution(14165357164633148941)
XLA Ops:
  0.6 0.0 copy-start
  0.6 3.1 %rotate.1 = (f32[384,1024]{1,0:T(8,128)S(1)}, f32[32,128]{1,0:T(8,128)S(1)}, bf16[256,256]{1,0:T(8,128)(2,1)S(1)}) custom-call(f32[384,1024]{1,0:T(8,128)} %bitcast.21, s32[384,1024]{1,0:T(8,128)} %flip_hbm.1, f32[384,1024]{1,0:T(8,128)} %bitcast.22), custom_call_target="tpu_custom_call" | custom-call | tf_op jit(solution)/shard_map/rotate/pallas_call | solution.py:174
  3.8 14.7 %all_to_all.37 = f32[32,1,128]{2,1,0:T(1,128)S(1)} all-to-all(f32[32,1,128]{2,1,0:T(1,128)S(1)} %bitcast.18), channel_id=1, replica_groups={{260,0,1,2,3,4,5,6,7,128,129,130,131,132,133,134,135,256,257,258,259,26..., dimensions={0} | all-to-all | bytes 32768 | tf_op jit(solution)/shard_map/all_to_all | solution.py:148
  18.4 0.1 reduce_max.9
  18.5 17.4 %all_to_all.38 = f32[16,1,128]{2,1,0:T(1,128)S(1)} all-to-all(f32[16,1,128]{2,1,0:T(1,128)S(1)} %broadcast_in_dim.10), channel_id=1, replica_groups={{80,16,8,24,0,32,40,120,48,112,56,104,64,96,72,88},{208,144,136,152,128..., dimensions={0} | all-to-all | bytes 16384 | tf_op jit(solution)/shard_map/all_to_all | solution.py:148
  35.9 0.0 copy-done
  35.9 5.5 %quantize.1 = (bf16[384,1024]{1,0:T(8,128)(2,1)S(1)}, f32[384,1024]{1,0:T(8,128)S(1)}, f32[8,128]{1,0:T(8,128)S(1)}, f32[1,1024]{1,0:T(1,128)S(1)}) custom-call(f32[16,128]{1,0:T(8,128)S(1)} %bitcast.17, f32[384,1024]{1,0:T(8,128)S(1)} %get-tuple-element.12.rot_ref, s32[1,16]{1,0:T(1,128)S(1)} %bitcast.20), custom_call_target="tpu_custom_call" | custom-call | tf_op jit(solution)/shard_map/quantize/pallas_call | solution.py:196
  41.3 14.4 %all_to_all.39.codes_ref = bf16[8,48,1024]{2,1,0:T(8,128)(2,1)S(1)} all-to-all(bf16[8,48,1024]{2,1,0:T(8,128)(2,1)S(1)} %bitcast.16), channel_id=1, replica_groups={{256,264,128,136,384,392,0,8},{272,280,144,152,400,408,16,24},{288,296,..., dimensions={0} | all-to-all | bytes 1572864 | tf_op jit(solution)/shard_map/all_to_all | solution.py:148
  55.8 0.3 partial.1
  56.1 0.7 convert_element_type.22
  56.8 12.0 %all-to-all-start.3 = ((f16[8,48,256]{2,1,0:T(8,128)(2,1)}), f16[8,48,256]{2,1,0:T(8,128)(2,1)S(1)}, u32[]{:S(2)}, u32[]{:S(2)}) async-start(f16[8,48,256]{2,1,0:T(8,128)(2,1)} %convert_element_type.22), calls=%async_computation.3 | async-start | bytes 393216 | tf_op jit(solution)/shard_map/all_to_all | solution.py:148
  68.8 1.8 %residual.1 = f32[384,1024]{1,0:T(8,128)} custom-call(f32[384,1024]{1,0:T(8,128)S(1)} %get-tuple-element.12.rot_ref, f32[384,1024]{1,0:T(8,128)S(1)} %get-tuple-element.15.full_ref, f32[8,128]{1,0:T(8,128)S(1)} %get-tuple-element.16.scale_ref), custom_call_target="tpu_custom_call" | custom-call | flops 786432 | bytes 4718592 | tf_op jit(solution)/shard_map/residual/pallas_call | solution.py:213
  70.6 5.3 %all-to-all-done.3 = f16[8,48,256]{2,1,0:T(8,128)(2,1)S(1)} async-done(((f16[8,48,256]{2,1,0:T(8,128)(2,1)}), f16[8,48,256]{2,1,0:T(8,128)(2,1)S(1)}, u32[]{:S(2)}, u32[]{:S(2)}) %all-to-all-start.3) | async-done | bytes 196640 | tf_op jit(solution)/shard_map/all_to_all | solution.py:148
  76.0 0.0 copy-start.1
  76.0 12.5 %all_to_all.40 = f16[4,48,256]{2,1,0:T(8,128)(2,1)S(1)} all-to-all(f16[4,48,256]{2,1,0:T(8,128)(2,1)S(1)} %broadcast_in_dim.11), channel_id=1, replica_groups={{64,32,80,48},{72,40,88,56},{192,160,208,176},{200,168,216,184},{320,28..., dimensions={0} | all-to-all | bytes 196608 | tf_op jit(solution)/shard_map/all_to_all | solution.py:148
  88.6 0.1 broadcast_in_dim.25
  88.6 12.2 %all_to_all.41 = f16[8,48,1024]{2,1,0:T(8,128)(2,1)S(1)} all-to-all(f16[8,48,1024]{2,1,0:T(8,128)(2,1)S(1)} %broadcast_in_dim.25), channel_id=1, replica_groups={{256,264,128,136,384,392,0,8},{272,280,144,152,400,408,16,24},{288,296,..., dimensions={0} | all-to-all | bytes 1572864 | tf_op jit(solution)/shard_map/all_to_all | solution.py:148
  100.8 0.0 copy-done.1
  100.8 1.5 %fusion = f32[384,1024]{1,0:T(8,128)} fusion(s32[384,1024]{1,0:T(8,128)S(1)} %copy-done.1, f16[8,48,1024]{2,1,0:T(8,128)(2,1)S(1)} %all_to_all.41, f32[1024]{0:T(1024)S(1)} %bitcast.19), kind=kLoop, calls=%fused_computation.1 | loop fusion | flops 1572864 | bytes 3936256 | tf_op jit(solution)/shard_map/mul | solution.py:240
  (5 shorter events, 0.1 us)
Async XLA Ops:
  0.6 35.2 %copy-start = (s32[16]{0:T(128)S(1)}, s32[16]{0:T(128)}, u32[]{:S(2)}) copy-start(s32[16]{0:T(128)} %param.7) | copy-start | bytes 196
  56.8 19.1 %all-to-all-start.3 = ((f16[8,48,256]{2,1,0:T(8,128)(2,1)}), f16[8,48,256]{2,1,0:T(8,128)(2,1)S(1)}, u32[]{:S(2)}, u32[]{:S(2)}) async-start(f16[8,48,256]{2,1,0:T(8,128)(2,1)} %convert_element_type.22), calls=%async_computation.3 | async-start | bytes 393216 | tf_op jit(solution)/shard_map/all_to_all | solution.py:148
  76.0 24.9 %copy-start.1 = (s32[384,1024]{1,0:T(8,128)S(1)}, s32[384,1024]{1,0:T(8,128)}, u32[]{:S(2)}) copy-start(s32[384,1024]{1,0:T(8,128)} %flip_hbm.1) | copy-start | bytes 4718596

commit v8 on v7

--- a/solution.py
+++ b/solution.py
@@ -158,7 +158,7 @@
         return sorted(range(depth), key=lambda z: (z != lead, -min((z - lead) % depth, (lead - z) % depth)))
 
     far_ring = by_distance(8)
-    near = [[y * depth + 2 * h + l for y in (2, 1, 3, 0) for l in range(2)] for h in pairs]
+    near = [[y * depth + 2 * h + l for y in (2, 0, 1, 3) for l in (1, 0)] for h in pairs]
     far = [[y * depth + z + l for z in far_ring if z % 2 == 0] for y in ys for l in range(2)]
     halves = ((8, 4, 10, 6), (14, 0, 2, 12))
     half = [[y * depth + z + l for z in members] for members in halves for y in ys for l in range(2)]

time: 103 us -> 103 us (level)
  no operation moved by 1% of the time
where the time goes in v8:
time: 103 us; the launch traced here: 102 us
  blocking collectives  70.7 us (69%)
  starting transfers between devices  12 us (12%)
  Pallas kernels  10.7 us (10%)
  waiting for transfers between devices  5.42 us (5%)
  other arithmetic  2.34 us (2%)
    all_to_all x5, blocking collectives, grouped(): return lax.all_to_all(pieces, axes, 0, 0, axis_index_groups=groups)  70.7 us
    all_to_all x1, starting transfers between devices, grouped(): return lax.all_to_all(pieces, axes, 0, 0, axis_index_groups=groups)  12 us
    pallas_call x1, Pallas kernels, on_device(): pl.pallas_call(functools.partial(quantize_kernel, replicas), in_specs=[vm...  5.46 us
    all_to_all x1, waiting for transfers between devices, grouped(): return lax.all_to_all(pieces, axes, 0, 0, axis_index_groups=groups)  5.42 us
    pallas_call x1, Pallas kernels, on_device(): pl.pallas_call(rotate_kernel, in_specs=[hbm] * 3, out_specs=[vmem] * 3, o...  3.11 us
  transfers between devices with their start and end apart: 1, of which 1 were waited for; matrix products, arithmetic and copies ran while one was open for 0% of the time, Pallas kernels for 2%

profile of v8, /device:TPU:6, one launch (start us, length us, event | category | flops | bytes accessed | tf_op | source)
XLA Modules:
  0.0 102.0 jit_solution(2680761534155841572)
XLA Ops:
  0.6 0.0 copy-start
  0.6 3.1 %rotate.1 = (f32[384,1024]{1,0:T(8,128)S(1)}, f32[32,128]{1,0:T(8,128)S(1)}, bf16[256,256]{1,0:T(8,128)(2,1)S(1)}) custom-call(f32[384,1024]{1,0:T(8,128)} %bitcast.21, s32[384,1024]{1,0:T(8,128)} %flip_hbm.1, f32[384,1024]{1,0:T(8,128)} %bitcast.22), custom_call_target="tpu_custom_call" | custom-call | tf_op jit(solution)/shard_map/rotate/pallas_call | solution.py:174
  3.8 14.7 %all_to_all.37 = f32[32,1,128]{2,1,0:T(1,128)S(1)} all-to-all(f32[32,1,128]{2,1,0:T(1,128)S(1)} %bitcast.18), channel_id=1, replica_groups={{260,0,1,2,3,4,5,6,7,128,129,130,131,132,133,134,135,256,257,258,259,26..., dimensions={0} | all-to-all | bytes 32768 | tf_op jit(solution)/shard_map/all_to_all | solution.py:148
  18.4 0.1 reduce_max.9
  18.5 17.4 %all_to_all.38 = f32[16,1,128]{2,1,0:T(1,128)S(1)} all-to-all(f32[16,1,128]{2,1,0:T(1,128)S(1)} %broadcast_in_dim.10), channel_id=1, replica_groups={{80,16,8,24,0,32,40,120,48,112,56,104,64,96,72,88},{208,144,136,152,128..., dimensions={0} | all-to-all | bytes 16384 | tf_op jit(solution)/shard_map/all_to_all | solution.py:148
  35.9 0.0 copy-done
  35.9 5.5 %quantize.1 = (bf16[384,1024]{1,0:T(8,128)(2,1)S(1)}, f32[384,1024]{1,0:T(8,128)S(1)}, f32[8,128]{1,0:T(8,128)S(1)}, f32[1,1024]{1,0:T(1,128)S(1)}) custom-call(f32[16,128]{1,0:T(8,128)S(1)} %bitcast.17, f32[384,1024]{1,0:T(8,128)S(1)} %get-tuple-element.12.rot_ref, s32[1,16]{1,0:T(1,128)S(1)} %bitcast.20), custom_call_target="tpu_custom_call" | custom-call | tf_op jit(solution)/shard_map/quantize/pallas_call | solution.py:196
  41.3 14.0 %all_to_all.39.codes_ref = bf16[8,48,1024]{2,1,0:T(8,128)(2,1)S(1)} all-to-all(bf16[8,48,1024]{2,1,0:T(8,128)(2,1)S(1)} %bitcast.16), channel_id=1, replica_groups={{264,256,8,0,136,128,392,384},{280,272,24,16,152,144,408,400},{296,288,..., dimensions={0} | all-to-all | bytes 1572864 | tf_op jit(solution)/shard_map/all_to_all | solution.py:148
  55.3 0.3 partial.1
  55.7 0.7 convert_element_type.22
  56.4 12.0 %all-to-all-start.3 = ((f16[8,48,256]{2,1,0:T(8,128)(2,1)}), f16[8,48,256]{2,1,0:T(8,128)(2,1)S(1)}, u32[]{:S(2)}, u32[]{:S(2)}) async-start(f16[8,48,256]{2,1,0:T(8,128)(2,1)} %convert_element_type.22), calls=%async_computation.3 | async-start | bytes 393216 | tf_op jit(solution)/shard_map/all_to_all | solution.py:148
  68.4 1.8 %residual.1 = f32[384,1024]{1,0:T(8,128)} custom-call(f32[384,1024]{1,0:T(8,128)S(1)} %get-tuple-element.12.rot_ref, f32[384,1024]{1,0:T(8,128)S(1)} %get-tuple-element.15.full_ref, f32[8,128]{1,0:T(8,128)S(1)} %get-tuple-element.16.scale_ref), custom_call_target="tpu_custom_call" | custom-call | flops 786432 | bytes 4718592 | tf_op jit(solution)/shard_map/residual/pallas_call | solution.py:213
  70.2 5.4 %all-to-all-done.3 = f16[8,48,256]{2,1,0:T(8,128)(2,1)S(1)} async-done(((f16[8,48,256]{2,1,0:T(8,128)(2,1)}), f16[8,48,256]{2,1,0:T(8,128)(2,1)S(1)}, u32[]{:S(2)}, u32[]{:S(2)}) %all-to-all-start.3) | async-done | bytes 196640 | tf_op jit(solution)/shard_map/all_to_all | solution.py:148
  75.6 0.0 copy-start.1
  75.7 11.6 %all_to_all.40 = f16[4,48,256]{2,1,0:T(8,128)(2,1)S(1)} all-to-all(f16[4,48,256]{2,1,0:T(8,128)(2,1)S(1)} %broadcast_in_dim.11), channel_id=1, replica_groups={{64,32,80,48},{72,40,88,56},{192,160,208,176},{200,168,216,184},{320,28..., dimensions={0} | all-to-all | bytes 196608 | tf_op jit(solution)/shard_map/all_to_all | solution.py:148
  87.3 0.1 broadcast_in_dim.25
  87.4 13.1 %all_to_all.41 = f16[8,48,1024]{2,1,0:T(8,128)(2,1)S(1)} all-to-all(f16[8,48,1024]{2,1,0:T(8,128)(2,1)S(1)} %broadcast_in_dim.25), channel_id=1, replica_groups={{264,256,8,0,136,128,392,384},{280,272,24,16,152,144,408,400},{296,288,..., dimensions={0} | all-to-all | bytes 1572864 | tf_op jit(solution)/shard_map/all_to_all | solution.py:148
  100.4 0.0 copy-done.1
  100.5 1.5 %fusion = f32[384,1024]{1,0:T(8,128)} fusion(s32[384,1024]{1,0:T(8,128)S(1)} %copy-done.1, f16[8,48,1024]{2,1,0:T(8,128)(2,1)S(1)} %all_to_all.41, f32[1024]{0:T(1024)S(1)} %bitcast.19), kind=kLoop, calls=%fused_computation.1 | loop fusion | flops 1572864 | bytes 3936256 | tf_op jit(solution)/shard_map/mul | solution.py:240
  (5 shorter events, 0.1 us)
Async XLA Ops:
  0.6 35.2 %copy-start = (s32[16]{0:T(128)S(1)}, s32[16]{0:T(128)}, u32[]{:S(2)}) copy-start(s32[16]{0:T(128)} %param.7) | copy-start | bytes 196
  56.4 19.2 %all-to-all-start.3 = ((f16[8,48,256]{2,1,0:T(8,128)(2,1)}), f16[8,48,256]{2,1,0:T(8,128)(2,1)S(1)}, u32[]{:S(2)}, u32[]{:S(2)}) async-start(f16[8,48,256]{2,1,0:T(8,128)(2,1)} %convert_element_type.22), calls=%async_computation.3 | async-start | bytes 393216 | tf_op jit(solution)/shard_map/all_to_all | solution.py:148
  75.6 24.8 %copy-start.1 = (s32[384,1024]{1,0:T(8,128)S(1)}, s32[384,1024]{1,0:T(8,128)}, u32[]{:S(2)}) copy-start(s32[384,1024]{1,0:T(8,128)} %flip_hbm.1) | copy-start | bytes 4718596

commit v9 on v7

--- a/solution.py
+++ b/solution.py
@@ -208,6 +208,19 @@
         name="quantize",
     )(peaks, rotated, level_table.reshape(1, levels))
 
+    first, second, third = len(near[0]), len(far[0]), len(half[0])
+    share = rows // first
+    codes = grouped(codes.reshape(first, share, width), "dp", near)
+    partial = pl.pallas_call(
+        functools.partial(partial_kernel, chunk_of),
+        out_shape=like((second, share, width // third), F32),
+        compiler_params=params(),
+        name="partial",
+    )(codes, matrix)
+    partial = grouped(partial.astype(F16), "dp", far)
+    partial, codes_full = lax.optimization_barrier((partial, full))
+    mean = jnp.sum(partial.astype(F32), axis=0) * 0.125
+    mean = jnp.broadcast_to(mean.astype(F16)[None], (third,) + mean.shape)
     block = 96
     tile = pl.BlockSpec((block, width), lambda i: (i, 0))
     new_residual = pl.pallas_call(
@@ -219,22 +232,9 @@
         compiler_params=params(),
         cost_estimate=pl.CostEstimate(flops=2 * rows * width, bytes_accessed=12 * rows * width, transcendentals=0),
         name="residual",
-    )(rotated, full, scale)
-
-    first, second, third = len(near[0]), len(far[0]), len(half[0])
-    share = rows // first
-    codes = grouped(codes.reshape(first, share, width), "dp", near)
-    partial = pl.pallas_call(
-        functools.partial(partial_kernel, chunk_of),
-        out_shape=like((second, share, width // third), F32),
-        compiler_params=params(),
-        name="partial",
-    )(codes, matrix)
-    partial = grouped(partial.astype(F16), "dp", far)
-    partial, new_residual = lax.optimization_barrier((partial, new_residual))
-    mean = jnp.sum(partial.astype(F32), axis=0) * 0.125
-    mean = jnp.broadcast_to(mean.astype(F16)[None], (third,) + mean.shape)
+    )(rotated, codes_full, scale)
     mean = grouped(mean, "dp", half)
+    mean, new_residual = lax.optimization_barrier((mean, new_residual))
     mean = mean.transpose(1, 0, 2).reshape(share, width)
     mean = grouped(jnp.broadcast_to(mean[None], (first, share, width)), "dp", near)
     mean = mean.reshape(rows, width).astype(F32) * factor * sign_flips.astype(F32)

time: 103 us -> 103 us (level)
  blocking collectives: 71.2 us -> 77.7 us
  starting transfers between devices: 12 us -> 7.04 us
  waiting for transfers between devices: 5.3 us -> 3.56 us
    all_to_all x5, blocking collectives: 71.2 us -> 77.7 us  [grouped(): return lax.all_to_all(pieces, axes, 0, 0, axis_index_groups=groups)]
    all_to_all x1, starting transfers between devices: 12 us -> 7.04 us  [grouped(): return lax.all_to_all(pieces, axes, 0, 0, axis_index_groups=groups)]
    all_to_all x1, waiting for transfers between devices: 5.3 us -> 3.56 us  [grouped(): return lax.all_to_all(pieces, axes, 0, 0, axis_index_groups=groups)]
where the time goes in v9:
time: 103 us; the launch traced here: 102 us
  blocking collectives  77.7 us (75%)
  Pallas kernels  10.7 us (10%)
  starting transfers between devices  7.04 us (7%)
  waiting for transfers between devices  3.56 us (3%)
  other arithmetic  1.56 us (2%)
    all_to_all x5, blocking collectives, grouped(): return lax.all_to_all(pieces, axes, 0, 0, axis_index_groups=groups)  77.7 us
    all_to_all x1, starting transfers between devices, grouped(): return lax.all_to_all(pieces, axes, 0, 0, axis_index_groups=groups)  7.04 us
    pallas_call x1, Pallas kernels, on_device(): pl.pallas_call(functools.partial(quantize_kernel, replicas), in_specs=[vm...  5.44 us
    all_to_all x1, waiting for transfers between devices, grouped(): return lax.all_to_all(pieces, axes, 0, 0, axis_index_groups=groups)  3.56 us
    pallas_call x1, Pallas kernels, on_device(): pl.pallas_call(rotate_kernel, in_specs=[hbm] * 3, out_specs=[vmem] * 3, o...  3.1 us
  transfers between devices with their start and end apart: 1, of which 1 were waited for; matrix products, arithmetic and copies ran while one was open for 0% of the time, Pallas kernels for 2%

profile of v9, /device:TPU:6, one launch (start us, length us, event | category | flops | bytes accessed | tf_op | source)
XLA Modules:
  0.0 102.0 jit_solution(17451964662726726642)
XLA Ops:
  0.6 0.0 copy-start
  0.6 3.1 %rotate.1 = (f32[384,1024]{1,0:T(8,128)S(1)}, f32[32,128]{1,0:T(8,128)S(1)}, bf16[256,256]{1,0:T(8,128)(2,1)S(1)}) custom-call(f32[384,1024]{1,0:T(8,128)} %bitcast.21, s32[384,1024]{1,0:T(8,128)} %flip_hbm.1, f32[384,1024]{1,0:T(8,128)} %bitcast.22), custom_call_target="tpu_custom_call" | custom-call | tf_op jit(solution)/shard_map/rotate/pallas_call | solution.py:174
  3.7 14.7 %all_to_all.37 = f32[32,1,128]{2,1,0:T(1,128)S(1)} all-to-all(f32[32,1,128]{2,1,0:T(1,128)S(1)} %bitcast.18), channel_id=1, replica_groups={{260,0,1,2,3,4,5,6,7,128,129,130,131,132,133,134,135,256,257,258,259,26..., dimensions={0} | all-to-all | bytes 32768 | tf_op jit(solution)/shard_map/all_to_all | solution.py:148
  18.4 0.1 reduce_max.9
  18.5 17.4 %all_to_all.38 = f32[16,1,128]{2,1,0:T(1,128)S(1)} all-to-all(f32[16,1,128]{2,1,0:T(1,128)S(1)} %broadcast_in_dim.10), channel_id=1, replica_groups={{80,16,8,24,0,32,40,120,48,112,56,104,64,96,72,88},{208,144,136,152,128..., dimensions={0} | all-to-all | bytes 16384 | tf_op jit(solution)/shard_map/all_to_all | solution.py:148
  35.8 0.0 copy-done
  35.8 5.4 %quantize.1 = (bf16[384,1024]{1,0:T(8,128)(2,1)S(1)}, f32[384,1024]{1,0:T(8,128)S(1)}, f32[8,128]{1,0:T(8,128)S(1)}, f32[1,1024]{1,0:T(1,128)S(1)}) custom-call(f32[16,128]{1,0:T(8,128)S(1)} %bitcast.17, f32[384,1024]{1,0:T(8,128)S(1)} %get-tuple-element.14.rot_ref, s32[1,16]{1,0:T(1,128)S(1)} %bitcast.20), custom_call_target="tpu_custom_call" | custom-call | tf_op jit(solution)/shard_map/quantize/pallas_call | solution.py:196
  41.3 14.4 %all_to_all.39.codes_ref = bf16[8,48,1024]{2,1,0:T(8,128)(2,1)S(1)} all-to-all(bf16[8,48,1024]{2,1,0:T(8,128)(2,1)S(1)} %bitcast.16), channel_id=1, replica_groups={{256,264,128,136,384,392,0,8},{272,280,144,152,400,408,16,24},{288,296,..., dimensions={0} | all-to-all | bytes 1572864 | tf_op jit(solution)/shard_map/all_to_all | solution.py:148
  55.7 0.3 partial.1
  56.1 18.7 %all_to_all.40 = f16[8,48,256]{2,1,0:T(8,128)(2,1)S(1)} all-to-all(f16[8,48,256]{2,1,0:T(8,128)(2,1)S(1)} %convert_element_type.22), channel_id=1, replica_groups={{64,0,16,112,32,96,48,80},{72,8,24,120,40,104,56,88},{192,128,144,240,1..., dimensions={0} | all-to-all | bytes 393216 | tf_op jit(solution)/shard_map/all_to_all | solution.py:148
  74.9 0.7 broadcast_in_dim.11
  75.5 7.0 %all-to-all-start.4 = ((f16[4,48,256]{2,1,0:T(8,128)(2,1)}), f16[4,48,256]{2,1,0:T(8,128)(2,1)S(1)}, u32[]{:S(2)}, u32[]{:S(2)}) async-start(f16[4,48,256]{2,1,0:T(8,128)(2,1)} %broadcast_in_dim.11), calls=%async_computation.4 | async-start | bytes 196608 | tf_op jit(solution)/shard_map/all_to_all | solution.py:148
  82.6 1.8 %residual.1 = f32[384,1024]{1,0:T(8,128)} custom-call(f32[384,1024]{1,0:T(8,128)S(1)} %get-tuple-element.14.rot_ref, f32[384,1024]{1,0:T(8,128)S(1)} %get-tuple-element.19.full_ref, f32[8,128]{1,0:T(8,128)S(1)} %get-tuple-element.20.scale_ref), custom_call_target="tpu_custom_call" | custom-call | flops 786432 | bytes 4718592 | tf_op jit(solution)/shard_map/residual/pallas_call | solution.py:226
  84.4 0.0 copy-start.1
  84.4 3.6 %all-to-all-done.4 = f16[4,48,256]{2,1,0:T(8,128)(2,1)S(1)} async-done(((f16[4,48,256]{2,1,0:T(8,128)(2,1)}), f16[4,48,256]{2,1,0:T(8,128)(2,1)S(1)}, u32[]{:S(2)}, u32[]{:S(2)}) %all-to-all-start.4) | async-done | bytes 98336 | tf_op jit(solution)/shard_map/all_to_all | solution.py:148
  88.0 0.1 broadcast_in_dim.25
  88.1 12.5 %all_to_all.41 = f16[8,48,1024]{2,1,0:T(8,128)(2,1)S(1)} all-to-all(f16[8,48,1024]{2,1,0:T(8,128)(2,1)S(1)} %broadcast_in_dim.25), channel_id=1, replica_groups={{256,264,128,136,384,392,0,8},{272,280,144,152,400,408,16,24},{288,296,..., dimensions={0} | all-to-all | bytes 1572864 | tf_op jit(solution)/shard_map/all_to_all | solution.py:148
  100.6 0.0 copy-done.1
  100.6 1.4 %fusion = f32[384,1024]{1,0:T(8,128)} fusion(s32[384,1024]{1,0:T(8,128)S(1)} %copy-done.1, f16[8,48,1024]{2,1,0:T(8,128)(2,1)S(1)} %all_to_all.41, f32[1024]{0:T(1024)S(1)} %bitcast.19), kind=kLoop, calls=%fused_computation.1 | loop fusion | flops 1572864 | bytes 3936256 | tf_op jit(solution)/shard_map/mul | solution.py:240
  (5 shorter events, 0.1 us)
Async XLA Ops:
  0.6 35.2 %copy-start = (s32[16]{0:T(128)S(1)}, s32[16]{0:T(128)}, u32[]{:S(2)}) copy-start(s32[16]{0:T(128)} %param.7) | copy-start | bytes 196
  75.5 12.4 %all-to-all-start.4 = ((f16[4,48,256]{2,1,0:T(8,128)(2,1)}), f16[4,48,256]{2,1,0:T(8,128)(2,1)S(1)}, u32[]{:S(2)}, u32[]{:S(2)}) async-start(f16[4,48,256]{2,1,0:T(8,128)(2,1)} %broadcast_in_dim.11), calls=%async_computation.4 | async-start | bytes 196608 | tf_op jit(solution)/shard_map/all_to_all | solution.py:148
  84.4 16.2 %copy-start.1 = (s32[384,1024]{1,0:T(8,128)S(1)}, s32[384,1024]{1,0:T(8,128)}, u32[]{:S(2)}) copy-start(s32[384,1024]{1,0:T(8,128)} %flip_hbm.1) | copy-start | bytes 4718596
